TPU v7x, 256 devices: a whole 4x4x8 slice. The times are simulated.
256 devices in a mesh: az: 16 (over x_lo, y, core), rad: 8 (over z), dep: 2 (over x_hi).
Axes of the slice: x: 4 (x_hi: 2, x_lo: 2; x = x_hi * 2 + x_lo), y: 4, z: 8, core: 2. Of those that a mesh axis runs over, the one named last changes fastest.
Arguments:
- forward_state: float32 [9, 256, 32, 256], P(None, 'az', 'rad', 'dep'), may hold values from -6 to 6
- forward_memory: float32 [3, 6, 256, 32, 256], P(None, None, 'az', 'rad', 'dep'), may hold values from -3 to 3
- adjoint_state: float32 [9, 256, 32, 256], P(None, 'az', 'rad', 'dep'), may hold values from -6 to 6
- adjoint_memory: float32 [3, 6, 256, 32, 256], P(None, None, 'az', 'rad', 'dep'), may hold values from -3 to 3
- shear_modulus: float32 [256, 32, 256], P('az', 'rad', 'dep'), may hold values from 0.5 to 2
- zone: int32 [256, 32, 256], P('az', 'rad', 'dep'), may hold values from 0 to 7
- zone_elastic: float32 [2, 8], replicated, may hold values from 0.5 to 2
- zone_rates: float32 [3, 8], replicated, may hold values from 0.25 to 4
- zone_weights: float32 [3, 8], replicated, may hold values from 0.1 to 1
- source_cells: int32 [16], replicated, may hold values from 0 to 2097151
- source_force: float32 [2, 3, 16], replicated, may hold values from -16 to 16
- receiver_cells: int32 [256], replicated, may hold values from 0 to 2097151
- receiver_residual: float32 [2, 3, 256], replicated, may hold values from -16 to 16
Outputs:
- gradient: float32 [256, 32, 256], P('az', 'rad', 'dep')
- adjoint_out: float32 [9, 256, 32, 256], P(None, 'az', 'rad', 'dep')
Inputs may be any that keep to these rules, and one draw needn't show every extreme that they name: `source_cells`: flat cell index (a * 32 + r) * 256 + z; cells may repeat. `receiver_cells`: flat cell index (a * 32 + r) * 256 + z; cells may repeat.
All inputs are finite; a program needn't handle non-finite values.
Results may differ from a plain program's by a relative error of at most 0.0003.
Values sent between devices are 32-bit elements; how exact they have to be, the bound alone decides.
A program may use at most 128 MiB of HBM per device.

v0:
```python
import math

import jax
import jax.numpy as jnp
from jax import lax
from jax.experimental import pallas as pl
from jax.experimental.pallas import tpu as pltpu
from jax.sharding import PartitionSpec as P

MESH = pl.DeviceIdType.MESH
f32 = jnp.float32

DT = 0.2
C1 = 1.125
C2 = 1.0 / 24.0

RR, RZ, RT, TT, TZ, ZZ = range(6)
IN_STATE = {RR: 3, TT: 4, ZZ: 5, RT: 6, RZ: 7, TZ: 8}
STRAIN_ORDER = (RR, TT, ZZ, RT, RZ, TZ)

ADJ, FWD = 0, 1
NAZ, NRAD, LANES = 16, 4, 128
LO, HI = 8, 8 + NAZ
R0 = 2


def forward4(before, here, after, after2):
    return C1 * (after - here) - C2 * (after2 - before)


def backward4(before2, before, here, after):
    return C1 * (here - before) - C2 * (after - before2)


def kernel(
    fs, fm, as_, am, mu_h, zone_h, ze_h, zr_h, zw_h, sc_h, sf_h, rc_h, rr_h,
    grad_h, adj_h,
    raw, mem, mu_v, zone_v, ze, zr, zw, sc_v, sf_v, rc_v, rr_v,
    stress, vel, dz, msg_out, msg_in, strain, a1, a2, inj, geo, mat, out_v, grad_v,
    in_sem, out_sem, send_sem, recv_sem,
):
    n_az, n_rad, n_dep = lax.axis_size("az"), lax.axis_size("rad"), lax.axis_size("dep")
    az, rad, dep = lax.axis_index("az"), lax.axis_index("rad"), lax.axis_index("dep")
    az_up, az_dn = {"az": lax.rem(az + 1, n_az)}, {"az": lax.rem(az + n_az - 1, n_az)}
    rad_up, rad_dn = {"rad": lax.rem(rad + 1, n_rad)}, {"rad": lax.rem(rad + n_rad - 1, n_rad)}
    dep_other = {"dep": 1 - dep}

    pending = []

    def bring(src, dst):
        copy = pltpu.make_async_copy(src, dst, in_sem.at[len(pending)])
        copy.start()
        pending.append(copy)
        return copy

    states = (as_, fs)
    memories = (am, fm)
    got_stress = [bring(states[s].at[pl.ds(3, 6)], raw.at[s, pl.ds(3, 6)]) for s in (ADJ, FWD)]

    barrier = pltpu.get_barrier_semaphore()
    for place in (az_up, az_dn, rad_up, rad_dn, dep_other):
        pl.semaphore_signal(barrier, inc=1, device_id=place, device_id_type=MESH)

    got_small = [
        bring(a, b)
        for a, b in (
            (ze_h, ze), (zr_h, zr), (zw_h, zw), (sc_h, sc_v), (sf_h, sf_v), (rc_h, rc_v),
            (rr_h, rr_v), (zone_h, zone_v), (mu_h, mu_v),
        )
    ]
    got_vel = [bring(states[s].at[pl.ds(0, 3)], raw.at[s, pl.ds(0, 3)]) for s in (ADJ, FWD)]
    got_mem = [bring(memories[s], mem.at[s]) for s in (ADJ, FWD)]

    lane = lax.broadcasted_iota(jnp.int32, (NAZ, LANES), 1)
    lane8 = lax.broadcasted_iota(jnp.int32, (8, LANES), 1)

    def where_f(cond, value):
        return jnp.where(cond, f32(value), f32(0.0))

    def pack_depth(sys, phase, fields):
        parcel = None
        for t, (get, ahead) in enumerate(fields):
            for r in range(NRAD):
                g = get(r)
                m1 = pltpu.roll(g, LANES - 1, 1)
                r1 = pltpu.roll(g, 1, 1)
                if ahead:
                    m2 = pltpu.roll(g, LANES - 2, 1)
                    stay = (where_f(lane < 127, C1) * m1 - C1 * g - where_f(lane < 126, C2) * m2
                            + where_f(lane >= 1, C2) * r1)
                    wrap = (where_f(lane == 127, C1) * m1 - where_f(lane >= 126, C2) * m2
                            + where_f(lane == 0, C2) * r1)
                else:
                    r2 = pltpu.roll(g, 2, 1)
                    stay = (C1 * g - where_f(lane >= 1, C1) * r1 - where_f(lane < 127, C2) * m1
                            + where_f(lane >= 2, C2) * r2)
                    wrap = (where_f(lane <= 1, C2) * r2 - where_f(lane == 0, C1) * r1
                            - where_f(lane == 127, C2) * m1)
                dz[sys, t, r] = stay
                for half in range(2):
                    shift = 12 * (2 * r + half) + 4 * t
                    piece = wrap[8 * half: 8 * half + 8]
                    if shift:
                        piece = pltpu.roll(piece, shift, 1)
                    parcel = piece if parcel is None else parcel + piece
        msg_out[sys, phase] = parcel

    mine = lane8 - 126 * (1 - dep)
    edge = (mine >= 0) & (mine < 2)

    def depth_diff(sys, parcel, t, r):
        halves = []
        for half in range(2):
            shift = 12 * (2 * r + half) + 4 * t
            piece = pltpu.roll(parcel, (LANES - shift) % LANES, 1) if shift else parcel
            halves.append(jnp.where(edge, piece, 0.0))
        return dz[sys, t, r] + jnp.concatenate(halves, axis=0)

    own = pl.ds(LO, NAZ)
    own_r = pl.ds(R0, NRAD)
    started = []

    def exchange(sys, phase, field, rad_plan, az_from, az_count):
        legs = []

        def leg(src, dst, place):
            number = len(legs)
            copy = pltpu.make_async_remote_copy(
                src_ref=src, dst_ref=dst, send_sem=send_sem.at[sys, phase, number],
                recv_sem=recv_sem.at[sys, phase, number], device_id=place, device_id_type=MESH,
            )
            copy.start()
            legs.append(copy)
            started.append(copy)

        comps = pl.ds(az_from, az_count)
        leg(field.at[comps, own_r, pl.ds(HI - 8, 8)], field.at[comps, own_r, pl.ds(0, 8)], az_up)
        leg(field.at[comps, own_r, pl.ds(LO, 8)], field.at[comps, own_r, pl.ds(HI, 8)], az_dn)
        for first, count, up, down in rad_plan:
            comps_r = pl.ds(first, count)
            leg(field.at[comps_r, pl.ds(R0 + NRAD - up, up), own],
                field.at[comps_r, pl.ds(R0 - up, up), own], rad_up)
            leg(field.at[comps_r, pl.ds(R0, down), own],
                field.at[comps_r, pl.ds(R0 + NRAD, down), own], rad_dn)
        leg(msg_out.at[sys, phase], msg_in.at[sys, phase], dep_other)
        return legs

    def arrive(legs, field, comps):
        for copy in legs:
            copy.wait_recv()

        @pl.when(rad == 0)
        def _():
            field[pl.ds(0, comps), pl.ds(0, R0), own] = jnp.zeros((comps, R0, NAZ, LANES), f32)

        @pl.when(rad == n_rad - 1)
        def _():
            field[pl.ds(0, comps), pl.ds(R0 + NRAD, 2), own] = jnp.zeros((comps, 2, NAZ, LANES), f32)

    def rows(r):
        return pl.ds(r, NAZ, stride=NRAD)

    def stress_field(sys, step):
        return stress.at[sys, step]

    def vel_field(sys, step):
        return vel.at[sys, step]

    def send_stress(sys, step):
        field = stress_field(sys, step)
        pack_depth(sys, 2 * step, [
            (lambda r: field[RZ, R0 + r, LO:HI], False),
            (lambda r: field[TZ, R0 + r, LO:HI], False),
            (lambda r: field[ZZ, R0 + r, LO:HI], True),
        ])
        return exchange(sys, 2 * step, field, ((RR, 1, 1, 2), (RZ, 2, 2, 1)), RT, 3)

    def send_vel(sys, step):
        field = vel_field(sys, step)
        pack_depth(sys, 2 * step + 1, [
            (lambda r: field[2, R0 + r, LO:HI], False),
            (lambda r: field[0, R0 + r, LO:HI], True),
            (lambda r: field[1, R0 + r, LO:HI], True),
        ])
        return exchange(sys, 2 * step + 1, field, ((0, 1, 2, 1), (1, 2, 1, 2)), 0, 3)

    def rad4(field, c, r, first):
        return [field[c, R0 + r + first + i, LO:HI] for i in range(4)]

    def az4(field, c, r, first):
        return [field[c, R0 + r, LO + first + i: HI + first + i] for i in range(4)]

    def velocity_update(sys, step):
        field, new = stress_field(sys, step), vel_field(sys, step)
        parcel = msg_in[sys, 2 * step]
        for r in range(NRAD):
            inv_s, inv_c, inv_sa, inv_ca = [geo[i, r] for i in range(4)]
            if step == 0:
                old = [raw[sys, c, rows(r)] for c in range(3)]
            else:
                old = [vel[sys, 0, c, R0 + r, LO:HI] for c in range(3)]
            s_rr, s_tt = field[RR, R0 + r, LO:HI], field[TT, R0 + r, LO:HI]
            s_rt, s_rz = field[RT, R0 + r, LO:HI], field[RZ, R0 + r, LO:HI]
            push = [
                forward4(*rad4(field, RR, r, -1)) + backward4(*az4(field, RT, r, -2)) * inv_sa
                + depth_diff(sys, parcel, 0, r) + (s_rr - s_tt) * inv_s,
                backward4(*rad4(field, RT, r, -2)) + forward4(*az4(field, TT, r, -1)) * inv_ca
                + depth_diff(sys, parcel, 1, r) + 2.0 * s_rt * inv_c,
                backward4(*rad4(field, RZ, r, -2)) + backward4(*az4(field, TZ, r, -2)) * inv_ca
                + depth_diff(sys, parcel, 2, r) + s_rz * inv_c,
            ]
            gain = mat[0, r]
            for c in range(3):
                new[c, R0 + r, LO:HI] = old[c] + gain * (push[c] + inj[sys, step, c, r])

    def strain_at(sys, step, parcel, r):
        field = vel_field(sys, step)
        inv_s, inv_c, inv_sa, inv_ca = [geo[i, r] for i in range(4)]
        v_r, v_t = field[0, R0 + r, LO:HI], field[1, R0 + r, LO:HI]
        return [
            backward4(*rad4(field, 0, r, -2)),
            backward4(*az4(field, 1, r, -2)) * inv_ca + v_r * inv_c,
            depth_diff(sys, parcel, 0, r),
            0.5 * (forward4(*rad4(field, 1, r, -1)) + forward4(*az4(field, 0, r, -1)) * inv_sa
                   - v_t * inv_s),
            0.5 * (depth_diff(sys, parcel, 1, r) + forward4(*rad4(field, 2, r, -1))),
            0.5 * (depth_diff(sys, parcel, 2, r) + forward4(*az4(field, 2, r, -1)) * inv_ca),
        ]

    def load_state(sys):
        got_stress[sys].wait()
        field = stress_field(sys, 0)
        for c in range(6):
            for r in range(NRAD):
                field[c, R0 + r, LO:HI] = raw[sys, IN_STATE[c], rows(r)]

    load_state(ADJ)
    pl.semaphore_wait(barrier, 5)
    legs_s = [None, None]
    legs_v = [None, None]
    legs_s[ADJ] = send_stress(ADJ, 0)
    load_state(FWD)
    legs_s[FWD] = send_stress(FWD, 0)

    for copy in got_small:
        copy.wait()
    angle = 2.0 * math.pi / (NAZ * n_az)
    inner = (NAZ * n_az) / (2.0 * math.pi)
    for r in range(NRAD):
        centre = jnp.full((NAZ, LANES), f32(inner), f32) + (rad * NRAD + r).astype(f32)
        staggered = centre + 0.5
        geo[0, r] = 1.0 / staggered
        geo[1, r] = 1.0 / centre
        geo[2, r] = 1.0 / (staggered * angle)
        geo[3, r] = 1.0 / (centre * angle)

    betas = []
    for r in range(NRAD):
        zone = zone_v[rows(r)]
        looked = [jnp.zeros((NAZ, LANES), f32) for _ in range(8)]
        for number in range(8):
            hit = zone == number
            for t in range(8):
                ref, row = (ze, t) if t < 2 else (zr, t - 2) if t < 5 else (zw, t - 5)
                looked[t] = jnp.where(hit, ref[row, number], looked[t])
        lame, buoyancy = looked[0], looked[1]
        alpha = [DT * looked[2 + i] for i in range(3)]
        weight = looked[5:8]
        beta = [1.0 - a for a in alpha]
        share = [a * w for a, w in zip(alpha, weight)]
        gain = DT * (1.0 - (share[0] + share[1] + share[2]))
        later = DT * (beta[0] * share[0] + beta[1] * share[1] + beta[2] * share[2])
        doubled = 2.0 * mu_v[rows(r)]
        mat[0, r] = DT * buoyancy
        mat[1, r] = gain * lame
        mat[2, r] = gain * doubled
        mat[3, r] = later * lame
        mat[4, r] = later * doubled
        for i in range(3):
            mat[5 + i, r] = beta[i]

    def inject(sys, cells_ref, force_ref, count):
        cells = cells_ref[...]
        around = lax.shift_right_logical(cells, 13) - NAZ * az
        radial = (lax.shift_right_logical(cells, 8) & 31) - NRAD * rad
        depth = (cells & 255) - LANES * dep
        inside = (around >= 0) & (around < NAZ) & (radial >= 0) & (radial < NRAD)
        key = jnp.where(inside, radial * NAZ + around, -1)
        here = lax.broadcasted_iota(jnp.int32, (NRAD * NAZ, count), 0) == key
        lanes = (lax.broadcasted_iota(jnp.int32, (LANES, count), 0) == depth).astype(f32)
        for step in range(2):
            for c in range(3):
                picked = jnp.where(here, force_ref[c, step: step + 1, :], 0.0)
                total = lax.dot_general(
                    picked, lanes, (((1,), (1,)), ((), ())),
                    precision=lax.Precision.HIGHEST, preferred_element_type=f32,
                )
                for r in range(NRAD):
                    inj[sys, step, c, r] = total[r * NAZ: (r + 1) * NAZ]

    inject(ADJ, rc_v, rr_v, rc_v.shape[1])
    inject(FWD, sc_v, sf_v, sc_v.shape[1])
    for sys in (ADJ, FWD):
        got_vel[sys].wait()

    def advance_velocity(sys, step):
        arrive(legs_s[sys], stress_field(sys, step), 3)
        velocity_update(sys, step)
        legs_v[sys] = send_vel(sys, step)

    for sys in (ADJ, FWD):
        advance_velocity(sys, 0)

    for sys in (ADJ, FWD):
        got_mem[sys].wait()
        for r in range(NRAD):
            beta = [mat[5 + i, r] for i in range(3)]
            for e in range(6):
                m = [beta[i] * mem[sys, 6 * i + e, rows(r)] for i in range(3)]
                a1[sys, e, r] = raw[sys, 3 + e, rows(r)] - DT * (m[0] + m[1] + m[2])
                if sys == ADJ:
                    a2[e, r] = DT * (beta[0] * m[0] + beta[1] * m[1] + beta[2] * m[2])

    def first_stress(sys):
        arrive(legs_v[sys], vel_field(sys, 0), 3)
        parcel = msg_in[sys, 1]
        new = stress_field(sys, 1)
        for r in range(NRAD):
            e = strain_at(sys, 0, parcel, r)
            dilation = e[0] + e[1] + e[2]
            common = mat[1, r] * dilation
            gm = mat[2, r]
            for i in range(6):
                strain[sys, 0, i, r] = e[i]
                change = gm * e[i] + common if i < 3 else gm * e[i]
                new[STRAIN_ORDER[i], R0 + r, LO:HI] = a1[sys, i, r] + change
        legs_s[sys] = send_stress(sys, 1)

    for sys in (ADJ, FWD):
        first_stress(sys)

    for r in range(NRAD):
        e = [strain[ADJ, 0, i, r] for i in range(6)]
        common = mat[3, r] * (e[0] + e[1] + e[2])
        hm = mat[4, r]
        for i in range(6):
            drop = hm * e[i] + common if i < 3 else hm * e[i]
            a2[i, r] = stress[ADJ, 1, STRAIN_ORDER[i], R0 + r, LO:HI] - a2[i, r] - drop

    for sys in (ADJ, FWD):
        advance_velocity(sys, 1)
    for r in range(NRAD):
        for c in range(3):
            out_v[c, rows(r)] = vel[ADJ, 1, c, R0 + r, LO:HI]
    out_vel = pltpu.make_async_copy(out_v.at[pl.ds(0, 3)], adj_h.at[pl.ds(0, 3)], out_sem.at[0])
    out_vel.start()

    def product(e, f):
        return 2.0 * DT * (e[0] * f[0] + e[1] * f[1] + e[2] * f[2]
                           + 2.0 * (e[3] * f[3] + e[4] * f[4] + e[5] * f[5]))

    arrive(legs_v[ADJ], vel_field(ADJ, 1), 3)
    parcel = msg_in[ADJ, 3]
    for r in range(NRAD):
        e = strain_at(ADJ, 1, parcel, r)
        common = mat[1, r] * (e[0] + e[1] + e[2])
        gm = mat[2, r]
        for i in range(6):
            change = gm * e[i] + common if i < 3 else gm * e[i]
            out_v[3 + i, rows(r)] = a2[i, r] + change
        a1[ADJ, 0, r] = product(e, [strain[FWD, 0, i, r] for i in range(6)])
    out_stress = pltpu.make_async_copy(out_v.at[pl.ds(3, 6)], adj_h.at[pl.ds(3, 6)], out_sem.at[1])
    out_stress.start()

    arrive(legs_v[FWD], vel_field(FWD, 1), 3)
    parcel = msg_in[FWD, 3]
    for r in range(NRAD):
        e = strain_at(FWD, 1, parcel, r)
        grad_v[rows(r)] = a1[ADJ, 0, r] + product(e, [strain[ADJ, 0, i, r] for i in range(6)])
    out_grad = pltpu.make_async_copy(grad_v, grad_h, out_sem.at[2])
    out_grad.start()

    for copy in started:
        copy.wait_send()
    out_vel.wait()
    out_stress.wait()
    out_grad.wait()


def shards(
    forward_state, forward_memory, adjoint_state, adjoint_memory, shear_modulus, zone,
    zone_elastic, zone_rates, zone_weights, source_cells, source_force, receiver_cells,
    receiver_residual,
):
    cells = NAZ * NRAD
    nsrc, nrec = source_cells.shape[0], receiver_cells.shape[0]
    block = (NRAD, NAZ, LANES)
    vmem = pltpu.VMEM
    hbm = pl.BlockSpec(memory_space=pltpu.HBM)
    gradient, adjoint_out = pl.pallas_call(
        kernel,
        out_shape=(
            jax.ShapeDtypeStruct((cells, LANES), f32),
            jax.ShapeDtypeStruct((9, cells, LANES), f32),
        ),
        in_specs=[hbm] * 13,
        out_specs=(hbm, hbm),
        scratch_shapes=[
            vmem((2, 9, cells, LANES), f32),
            vmem((2, 18, cells, LANES), f32),
            vmem((cells, LANES), f32),
            vmem((cells, LANES), jnp.int32),
            pltpu.SMEM((2, 8), f32),
            pltpu.SMEM((3, 8), f32),
            pltpu.SMEM((3, 8), f32),
            vmem((1, nsrc), jnp.int32),
            vmem((3, 2, nsrc), f32),
            vmem((1, nrec), jnp.int32),
            vmem((3, 2, nrec), f32),
            vmem((2, 2, 6, NRAD + 4, NAZ + 16, LANES), f32),
            vmem((2, 2, 3, NRAD + 4, NAZ + 16, LANES), f32),
            vmem((2, 3) + block, f32),
            vmem((2, 4, 8, LANES), f32),
            vmem((2, 4, 8, LANES), f32),
            vmem((2, 1, 6) + block, f32),
            vmem((2, 6) + block, f32),
            vmem((6,) + block, f32),
            vmem((2, 2, 3) + block, f32),
            vmem((4,) + block, f32),
            vmem((8,) + block, f32),
            vmem((9, cells, LANES), f32),
            vmem((cells, LANES), f32),
            pltpu.SemaphoreType.DMA((16,)),
            pltpu.SemaphoreType.DMA((3,)),
            pltpu.SemaphoreType.DMA((2, 4, 7)),
            pltpu.SemaphoreType.DMA((2, 4, 7)),
        ],
        compiler_params=pltpu.CompilerParams(
            collective_id=0, has_side_effects=True, vmem_limit_bytes=60 * 2**20
        ),
        name="window",
    )(
        forward_state.reshape(9, cells, LANES),
        forward_memory.reshape(18, cells, LANES),
        adjoint_state.reshape(9, cells, LANES),
        adjoint_memory.reshape(18, cells, LANES),
        shear_modulus.reshape(cells, LANES),
        zone.reshape(cells, LANES),
        zone_elastic, zone_rates, zone_weights,
        source_cells.reshape(1, nsrc), source_force.transpose(1, 0, 2),
        receiver_cells.reshape(1, nrec), receiver_residual.transpose(1, 0, 2),
    )
    return gradient.reshape(NAZ, NRAD, LANES), adjoint_out.reshape(9, NAZ, NRAD, LANES)


def solution(mesh):
    return jax.shard_map(
        shards,
        mesh=mesh,
        in_specs=(
            P(None, "az", "rad", "dep"),
            P(None, None, "az", "rad", "dep"),
            P(None, "az", "rad", "dep"),
            P(None, None, "az", "rad", "dep"),
            P("az", "rad", "dep"),
            P("az", "rad", "dep"),
            P(), P(), P(), P(), P(), P(), P(),
        ),
        out_specs=(P("az", "rad", "dep"), P(None, "az", "rad", "dep")),
        check_vma=False,
    )
```

profile of v0, /device:TPU:1, one launch (start us, length us, event | category | flops | bytes accessed | tf_op | source)
XLA Modules:
  0.0 30.2 jit_solution(3116097635852629099)
XLA Ops:
  0.6 26.5 %window.1 = (f32[64,128]{1,0:T(8,128)}, f32[9,64,128]{2,1,0:T(8,128)}) custom-call(f32[9,64,128]{2,1,0:T(8,128)} %bitcast.15, f32[18,64,128]{2,1,0:T(8,128)} %bitcast.12, f32[9,64,128]{2,1,0:T(8,128)} %bitcast.16, f32[18,64,128]{2,1,0:T(8,128)} %bitcast.13, f32[64,128]{1,0:T(8,128)} %bitcast.17, s32[64,128]{1,0:T(8,128)} %bitcast.18, f32[2,8]{1,0:T(2,128)} %ze_h.1, ...), custom_call_target="tpu_custom_call" | custom-call | tf_op jit(solution)/shard_map/window/pallas_call | solution.py:400
  27.1 1.4 %copy.17 = f32[16,4,128]{2,1,0:T(4,128)} copy(f32[16,4,128]{2,1,0:T(4,128)} %bitcast.19) | data formatting | bytes 65536
  28.5 1.7 %copy.18 = f32[9,16,4,128]{3,2,1,0:T(4,128)} copy(f32[9,16,4,128]{3,2,1,0:T(4,128)} %bitcast.14) | data formatting | bytes 589824
where the time goes:
time: 30.4 us; the launch traced here: 30.2 us
  Pallas kernels  26.5 us (87%)
  local copies, waits for them, and re-layouts  3.07 us (10%)
  between operations  0.64 us (2%)
    pallas_call x1, Pallas kernels, shards(): pl.pallas_call(kernel, out_shape=(jax.ShapeDtypeStruct((cells, LANES), f3...  26.5 us
    unnamed x2, local copies, waits for them, and re-layouts  3.07 us

commit v1 on v0

--- a/solution.py
+++ b/solution.py
@@ -22,6 +22,20 @@
 NAZ, NRAD, LANES = 16, 4, 128
 LO, HI = 8, 8 + NAZ
 R0 = 2
+
+
+class View:
+    def __init__(self, ref, sys, step):
+        self.ref, self.lead = ref, (sys, step)
+
+    def __getitem__(self, index):
+        return self.ref[self.lead + index]
+
+    def __setitem__(self, index, value):
+        self.ref[self.lead + index] = value
+
+    def slab(self, index):
+        return self.ref.at[self.lead + index]
 
 
 def forward4(before, here, after, after2):
@@ -42,8 +56,21 @@
     n_az, n_rad, n_dep = lax.axis_size("az"), lax.axis_size("rad"), lax.axis_size("dep")
     az, rad, dep = lax.axis_index("az"), lax.axis_index("rad"), lax.axis_index("dep")
     az_up, az_dn = {"az": lax.rem(az + 1, n_az)}, {"az": lax.rem(az + n_az - 1, n_az)}
-    rad_up, rad_dn = {"rad": lax.rem(rad + 1, n_rad)}, {"rad": lax.rem(rad + n_rad - 1, n_rad)}
+    rad_up, rad_dn = {"rad": rad + 1}, {"rad": rad - 1}
     dep_other = {"dep": 1 - dep}
+
+    has_dn, has_up = rad > 0, rad < n_rad - 1
+    barrier = pltpu.get_barrier_semaphore()
+    for place in (az_up, az_dn, dep_other):
+        pl.semaphore_signal(barrier, inc=1, device_id=place, device_id_type=MESH)
+
+    @pl.when(has_up)
+    def _():
+        pl.semaphore_signal(barrier, inc=1, device_id=rad_up, device_id_type=MESH)
+
+    @pl.when(has_dn)
+    def _():
+        pl.semaphore_signal(barrier, inc=1, device_id=rad_dn, device_id_type=MESH)
 
     pending = []
 
@@ -56,10 +83,6 @@
     states = (as_, fs)
     memories = (am, fm)
     got_stress = [bring(states[s].at[pl.ds(3, 6)], raw.at[s, pl.ds(3, 6)]) for s in (ADJ, FWD)]
-
-    barrier = pltpu.get_barrier_semaphore()
-    for place in (az_up, az_dn, rad_up, rad_dn, dep_other):
-        pl.semaphore_signal(barrier, inc=1, device_id=place, device_id_type=MESH)
 
     got_small = [
         bring(a, b)
@@ -77,33 +100,57 @@
     def where_f(cond, value):
         return jnp.where(cond, f32(value), f32(0.0))
 
-    def pack_depth(sys, phase, fields):
+    def base(t, r, half):
+        return 12 * (2 * r + half) + 4 * t
+
+    ends = (lane8 < 2) | (lane8 >= 126)
+
+    def pack_depth(sys, phase, gets):
         parcel = None
-        for t, (get, ahead) in enumerate(fields):
+        for r in range(NRAD):
+            for t, get in enumerate(gets):
+                g = get(r)
+                for half in range(2):
+                    piece = jnp.where(ends, g[8 * half: 8 * half + 8], 0.0)
+                    if base(t, r, half):
+                        piece = pltpu.roll(piece, base(t, r, half), 1)
+                    parcel = piece if parcel is None else parcel + piece
+        msg_out[sys, phase] = parcel
+
+    def local_depth(sys, gets, aheads):
+        for t in range(3):
             for r in range(NRAD):
-                g = get(r)
+                g = gets[t](r)
                 m1 = pltpu.roll(g, LANES - 1, 1)
                 r1 = pltpu.roll(g, 1, 1)
-                if ahead:
+                if aheads[t]:
                     m2 = pltpu.roll(g, LANES - 2, 1)
-                    stay = (where_f(lane < 127, C1) * m1 - C1 * g - where_f(lane < 126, C2) * m2
-                            + where_f(lane >= 1, C2) * r1)
-                    wrap = (where_f(lane == 127, C1) * m1 - where_f(lane >= 126, C2) * m2
-                            + where_f(lane == 0, C2) * r1)
+                    dz[sys, t, r] = (where_f(lane < 127, C1) * m1 - C1 * g - where_f(lane < 126, C2) * m2
+                                     + where_f(lane >= 1, C2) * r1)
                 else:
                     r2 = pltpu.roll(g, 2, 1)
-                    stay = (C1 * g - where_f(lane >= 1, C1) * r1 - where_f(lane < 127, C2) * m1
-                            + where_f(lane >= 2, C2) * r2)
-                    wrap = (where_f(lane <= 1, C2) * r2 - where_f(lane == 0, C1) * r1
-                            - where_f(lane == 127, C2) * m1)
-                dz[sys, t, r] = stay
-                for half in range(2):
-                    shift = 12 * (2 * r + half) + 4 * t
-                    piece = wrap[8 * half: 8 * half + 8]
-                    if shift:
-                        piece = pltpu.roll(piece, shift, 1)
-                    parcel = piece if parcel is None else parcel + piece
-        msg_out[sys, phase] = parcel
+                    dz[sys, t, r] = (C1 * g - where_f(lane >= 1, C1) * r1 - where_f(lane < 127, C2) * m1
+                                     + where_f(lane >= 2, C2) * r2)
+
+    slot = lax.rem(lax.rem(lane8 + 2, LANES), 12)
+    place_in = lax.rem(slot, 4)
+    which = lax.div(slot, 4)
+
+    def wraps(sys, phase, aheads):
+        x = msg_in[sys, phase]
+        ahead = None
+        for t in range(3):
+            if aheads[t]:
+                ahead = (which == t) if ahead is None else ahead | (which == t)
+        behind = jnp.logical_not(ahead)
+        m1, m2 = pltpu.roll(x, LANES - 1, 1), pltpu.roll(x, LANES - 2, 1)
+        r1, r2 = pltpu.roll(x, 1, 1), pltpu.roll(x, 2, 1)
+        at126, at127, at0, at1 = [place_in == i for i in range(4)]
+        k_m1 = jnp.where(at127, jnp.where(ahead, f32(C1), f32(-C2)), 0.0)
+        k_m2 = where_f(ahead & (at126 | at127), -C2)
+        k_r1 = jnp.where(at0, jnp.where(ahead, f32(C2), f32(-C1)), 0.0)
+        k_r2 = where_f(behind & (at0 | at1), C2)
+        return k_m1 * m1 + k_m2 * m2 + k_r1 * r1 + k_r2 * r2
 
     mine = lane8 - 126 * (1 - dep)
     edge = (mine >= 0) & (mine < 2)
@@ -111,8 +158,8 @@
     def depth_diff(sys, parcel, t, r):
         halves = []
         for half in range(2):
-            shift = 12 * (2 * r + half) + 4 * t
-            piece = pltpu.roll(parcel, (LANES - shift) % LANES, 1) if shift else parcel
+            shift = base(t, r, half)
+            piece = pltpu.roll(parcel, LANES - shift, 1) if shift else parcel
             halves.append(jnp.where(edge, piece, 0.0))
         return dz[sys, t, r] + jnp.concatenate(halves, axis=0)
 
@@ -121,68 +168,97 @@
     started = []
 
     def exchange(sys, phase, field, rad_plan, az_from, az_count):
-        legs = []
-
-        def leg(src, dst, place):
-            number = len(legs)
-            copy = pltpu.make_async_remote_copy(
-                src_ref=src, dst_ref=dst, send_sem=send_sem.at[sys, phase, number],
-                recv_sem=recv_sem.at[sys, phase, number], device_id=place, device_id_type=MESH,
+        number = [0]
+        legs, up_legs, dn_legs = [], [], []
+
+        def leg(where, src, dst, place, group):
+            n = number[0]
+            number[0] += 1
+
+            def make():
+                return pltpu.make_async_remote_copy(
+                    src_ref=where.slab(src), dst_ref=where.slab(dst),
+                    send_sem=send_sem.at[sys, phase, n], recv_sem=recv_sem.at[sys, phase, n],
+                    device_id=place, device_id_type=MESH,
+                )
+
+            make().start()
+            group.append(make)
+
+        @pl.when(has_up)
+        def _():
+            for first, count, up, down in rad_plan:
+                comps = pl.ds(first, count)
+                leg(field, (comps, pl.ds(R0 + NRAD - up, up), own), (comps, pl.ds(R0 - up, up), own),
+                    rad_up, up_legs)
+
+        @pl.when(has_dn)
+        def _():
+            for first, count, up, down in rad_plan:
+                comps = pl.ds(first, count)
+                leg(field, (comps, pl.ds(R0, down), own), (comps, pl.ds(R0 + NRAD, down), own),
+                    rad_dn, dn_legs)
+
+        comps = pl.ds(az_from, az_count)
+        leg(field, (comps, own_r, pl.ds(HI - 8, 8)), (comps, own_r, pl.ds(0, 8)), az_up, legs)
+        leg(field, (comps, own_r, pl.ds(LO, 8)), (comps, own_r, pl.ds(HI, 8)), az_dn, legs)
+        legs_msg = number[0]
+
+        def make_depth():
+            return pltpu.make_async_remote_copy(
+                src_ref=msg_out.at[sys, phase], dst_ref=msg_in.at[sys, phase],
+                send_sem=send_sem.at[sys, phase, legs_msg], recv_sem=recv_sem.at[sys, phase, legs_msg],
+                device_id=dep_other, device_id_type=MESH,
             )
-            copy.start()
-            legs.append(copy)
-            started.append(copy)
-
-        comps = pl.ds(az_from, az_count)
-        leg(field.at[comps, own_r, pl.ds(HI - 8, 8)], field.at[comps, own_r, pl.ds(0, 8)], az_up)
-        leg(field.at[comps, own_r, pl.ds(LO, 8)], field.at[comps, own_r, pl.ds(HI, 8)], az_dn)
-        for first, count, up, down in rad_plan:
-            comps_r = pl.ds(first, count)
-            leg(field.at[comps_r, pl.ds(R0 + NRAD - up, up), own],
-                field.at[comps_r, pl.ds(R0 - up, up), own], rad_up)
-            leg(field.at[comps_r, pl.ds(R0, down), own],
-                field.at[comps_r, pl.ds(R0 + NRAD, down), own], rad_dn)
-        leg(msg_out.at[sys, phase], msg_in.at[sys, phase], dep_other)
-        return legs
-
-    def arrive(legs, field, comps):
-        for copy in legs:
-            copy.wait_recv()
-
-        @pl.when(rad == 0)
+
+        make_depth().start()
+        legs.append(make_depth)
+        groups = legs, up_legs, dn_legs
+        started.append(groups)
+        return groups
+
+    def arrive(groups):
+        legs, up_legs, dn_legs = groups
+        for make in legs:
+            make().wait_recv()
+
+        @pl.when(has_dn)
         def _():
-            field[pl.ds(0, comps), pl.ds(0, R0), own] = jnp.zeros((comps, R0, NAZ, LANES), f32)
-
-        @pl.when(rad == n_rad - 1)
+            for make in up_legs:
+                make().wait_recv()
+
+        @pl.when(has_up)
         def _():
-            field[pl.ds(0, comps), pl.ds(R0 + NRAD, 2), own] = jnp.zeros((comps, 2, NAZ, LANES), f32)
+            for make in dn_legs:
+                make().wait_recv()
 
     def rows(r):
         return pl.ds(r, NAZ, stride=NRAD)
 
     def stress_field(sys, step):
-        return stress.at[sys, step]
+        return View(stress, sys, step)
 
     def vel_field(sys, step):
-        return vel.at[sys, step]
+        return View(vel, sys, step)
+
+    STRESS_AHEAD = (False, False, True)
+    VEL_AHEAD = (False, True, True)
 
     def send_stress(sys, step):
         field = stress_field(sys, step)
-        pack_depth(sys, 2 * step, [
-            (lambda r: field[RZ, R0 + r, LO:HI], False),
-            (lambda r: field[TZ, R0 + r, LO:HI], False),
-            (lambda r: field[ZZ, R0 + r, LO:HI], True),
-        ])
-        return exchange(sys, 2 * step, field, ((RR, 1, 1, 2), (RZ, 2, 2, 1)), RT, 3)
+        gets = [lambda r, c=c: field[c, R0 + r, LO:HI] for c in (RZ, TZ, ZZ)]
+        pack_depth(sys, 2 * step, gets)
+        groups = exchange(sys, 2 * step, field, ((RR, 1, 1, 2), (RZ, 2, 2, 1)), RT, 3)
+        local_depth(sys, gets, STRESS_AHEAD)
+        return groups
 
     def send_vel(sys, step):
         field = vel_field(sys, step)
-        pack_depth(sys, 2 * step + 1, [
-            (lambda r: field[2, R0 + r, LO:HI], False),
-            (lambda r: field[0, R0 + r, LO:HI], True),
-            (lambda r: field[1, R0 + r, LO:HI], True),
-        ])
-        return exchange(sys, 2 * step + 1, field, ((0, 1, 2, 1), (1, 2, 1, 2)), 0, 3)
+        gets = [lambda r, c=c: field[c, R0 + r, LO:HI] for c in (2, 0, 1)]
+        pack_depth(sys, 2 * step + 1, gets)
+        groups = exchange(sys, 2 * step + 1, field, ((0, 1, 2, 1), (1, 2, 1, 2)), 0, 3)
+        local_depth(sys, gets, VEL_AHEAD)
+        return groups
 
     def rad4(field, c, r, first):
         return [field[c, R0 + r + first + i, LO:HI] for i in range(4)]
@@ -192,7 +268,7 @@
 
     def velocity_update(sys, step):
         field, new = stress_field(sys, step), vel_field(sys, step)
-        parcel = msg_in[sys, 2 * step]
+        parcel = wraps(sys, 2 * step, STRESS_AHEAD)
         for r in range(NRAD):
             inv_s, inv_c, inv_sa, inv_ca = [geo[i, r] for i in range(4)]
             if step == 0:
@@ -235,12 +311,26 @@
                 field[c, R0 + r, LO:HI] = raw[sys, IN_STATE[c], rows(r)]
 
     load_state(ADJ)
-    pl.semaphore_wait(barrier, 5)
+    pl.semaphore_wait(barrier, 3 + has_up.astype(jnp.int32) + has_dn.astype(jnp.int32))
     legs_s = [None, None]
     legs_v = [None, None]
     legs_s[ADJ] = send_stress(ADJ, 0)
     load_state(FWD)
     legs_s[FWD] = send_stress(FWD, 0)
+
+    @pl.when(rad == 0)
+    def _():
+        for sys in (ADJ, FWD):
+            for step in range(2):
+                stress[sys, step, 0:3, 0:R0, LO:HI] = jnp.zeros((3, R0, NAZ, LANES), f32)
+                vel[sys, step, :, 0:R0, LO:HI] = jnp.zeros((3, R0, NAZ, LANES), f32)
+
+    @pl.when(rad == n_rad - 1)
+    def _():
+        for sys in (ADJ, FWD):
+            for step in range(2):
+                stress[sys, step, 0:3, R0 + NRAD:, LO:HI] = jnp.zeros((3, 2, NAZ, LANES), f32)
+                vel[sys, step, :, R0 + NRAD:, LO:HI] = jnp.zeros((3, 2, NAZ, LANES), f32)
 
     for copy in got_small:
         copy.wait()
@@ -304,7 +394,7 @@
         got_vel[sys].wait()
 
     def advance_velocity(sys, step):
-        arrive(legs_s[sys], stress_field(sys, step), 3)
+        arrive(legs_s[sys])
         velocity_update(sys, step)
         legs_v[sys] = send_vel(sys, step)
 
@@ -322,8 +412,8 @@
                     a2[e, r] = DT * (beta[0] * m[0] + beta[1] * m[1] + beta[2] * m[2])
 
     def first_stress(sys):
-        arrive(legs_v[sys], vel_field(sys, 0), 3)
-        parcel = msg_in[sys, 1]
+        arrive(legs_v[sys])
+        parcel = wraps(sys, 1, VEL_AHEAD)
         new = stress_field(sys, 1)
         for r in range(NRAD):
             e = strain_at(sys, 0, parcel, r)
@@ -359,8 +449,8 @@
         return 2.0 * DT * (e[0] * f[0] + e[1] * f[1] + e[2] * f[2]
                            + 2.0 * (e[3] * f[3] + e[4] * f[4] + e[5] * f[5]))
 
-    arrive(legs_v[ADJ], vel_field(ADJ, 1), 3)
-    parcel = msg_in[ADJ, 3]
+    arrive(legs_v[ADJ])
+    parcel = wraps(ADJ, 3, VEL_AHEAD)
     for r in range(NRAD):
         e = strain_at(ADJ, 1, parcel, r)
         common = mat[1, r] * (e[0] + e[1] + e[2])
@@ -372,19 +462,44 @@
     out_stress = pltpu.make_async_copy(out_v.at[pl.ds(3, 6)], adj_h.at[pl.ds(3, 6)], out_sem.at[1])
     out_stress.start()
 
-    arrive(legs_v[FWD], vel_field(FWD, 1), 3)
-    parcel = msg_in[FWD, 3]
+    arrive(legs_v[FWD])
+    parcel = wraps(FWD, 3, VEL_AHEAD)
     for r in range(NRAD):
         e = strain_at(FWD, 1, parcel, r)
         grad_v[rows(r)] = a1[ADJ, 0, r] + product(e, [strain[ADJ, 0, i, r] for i in range(6)])
     out_grad = pltpu.make_async_copy(grad_v, grad_h, out_sem.at[2])
     out_grad.start()
 
-    for copy in started:
-        copy.wait_send()
+    for legs, up_legs, dn_legs in started:
+        for make in legs:
+            make().wait_send()
+
+    @pl.when(has_up)
+    def _():
+        for _, up_legs, _ in started:
+            for make in up_legs:
+                make().wait_send()
+
+    @pl.when(has_dn)
+    def _():
+        for _, _, dn_legs in started:
+            for make in dn_legs:
+                make().wait_send()
+
     out_vel.wait()
     out_stress.wait()
     out_grad.wait()
+
+
+def hand_on(grad_in, adj_in, grad_out, adj_out, sems):
+    copies = [
+        pltpu.make_async_copy(adj_in.at[pl.ds(3 * i, 3)], adj_out.at[pl.ds(3 * i, 3)], sems.at[i])
+        for i in range(3)
+    ] + [pltpu.make_async_copy(grad_in, grad_out, sems.at[3])]
+    for copy in copies:
+        copy.start()
+    for copy in copies:
+        copy.wait()
 
 
 def shards(
@@ -450,6 +565,18 @@
         source_cells.reshape(1, nsrc), source_force.transpose(1, 0, 2),
         receiver_cells.reshape(1, nrec), receiver_residual.transpose(1, 0, 2),
     )
+    gradient, adjoint_out = pl.pallas_call(
+        hand_on,
+        out_shape=(
+            jax.ShapeDtypeStruct((cells, LANES), f32),
+            jax.ShapeDtypeStruct((9, cells, LANES), f32),
+        ),
+        in_specs=[hbm, hbm],
+        out_specs=(hbm, hbm),
+        scratch_shapes=[pltpu.SemaphoreType.DMA((4,))],
+        compiler_params=pltpu.CompilerParams(vmem_limit_bytes=60 * 2**20),
+        name="hand_on",
+    )(gradient, adjoint_out)
     return gradient.reshape(NAZ, NRAD, LANES), adjoint_out.reshape(9, NAZ, NRAD, LANES)
 
 

time: 30.4 us -> 36.6 us (1.20)
  the two profiles are of different devices: /device:TPU:1 before, /device:TPU:32 now
where the time goes in v1:
time: 36.6 us; the launch traced here: 36.3 us
  Pallas kernels  35.7 us (98%)
  between operations  0.64 us (2%)
    pallas_call x1, Pallas kernels, shards(): pl.pallas_call(kernel, out_shape=(jax.ShapeDtypeStruct((cells, LANES), f3...  24.6 us
    pallas_call x1, Pallas kernels, shards(): pl.pallas_call(hand_on, out_shape=(jax.ShapeDtypeStruct((cells, LANES), f...  11.1 us

profile of v1, /device:TPU:32, one launch (start us, length us, event | category | flops | bytes accessed | tf_op | source)
XLA Modules:
  0.0 36.3 jit_solution(8556841236300069215)
XLA Ops:
  0.6 24.6 %window.1 = (f32[64,128]{1,0:T(8,128)}, f32[9,64,128]{2,1,0:T(8,128)}) custom-call(f32[9,64,128]{2,1,0:T(8,128)} %bitcast.14, f32[18,64,128]{2,1,0:T(8,128)} %bitcast.12, f32[9,64,128]{2,1,0:T(8,128)} %bitcast.15, f32[18,64,128]{2,1,0:T(8,128)} %bitcast.13, f32[64,128]{1,0:T(8,128)} %bitcast.16, s32[64,128]{1,0:T(8,128)} %bitcast.17, f32[2,8]{1,0:T(2,128)} %ze_h.1, ...), custom_call_target="tpu_custom_call" | custom-call | tf_op jit(solution)/shard_map/window/pallas_call | solution.py:515
  25.3 11.1 %hand_on.1 = (f32[64,128]{1,0:T(8,128)}, f32[9,64,128]{2,1,0:T(8,128)}) custom-call(f32[64,128]{1,0:T(8,128)} %get-tuple-element.6.grad_in, f32[9,64,128]{2,1,0:T(8,128)} %get-tuple-element.7.adj_in), custom_call_target="tpu_custom_call" | custom-call | tf_op jit(solution)/shard_map/hand_on/pallas_call | solution.py:568

commit v2 on v1

--- a/solution.py
+++ b/solution.py
@@ -48,10 +48,10 @@
 
 def kernel(
     fs, fm, as_, am, mu_h, zone_h, ze_h, zr_h, zw_h, sc_h, sf_h, rc_h, rr_h,
-    grad_h, adj_h,
+    grad_v, out_v,
     raw, mem, mu_v, zone_v, ze, zr, zw, sc_v, sf_v, rc_v, rr_v,
-    stress, vel, dz, msg_out, msg_in, strain, a1, a2, inj, geo, mat, out_v, grad_v,
-    in_sem, out_sem, send_sem, recv_sem,
+    stress, vel, dz, msg_out, msg_in, strain, a1, a2, inj, geo, mat,
+    in_sem, send_sem, recv_sem,
 ):
     n_az, n_rad, n_dep = lax.axis_size("az"), lax.axis_size("rad"), lax.axis_size("dep")
     az, rad, dep = lax.axis_index("az"), lax.axis_index("rad"), lax.axis_index("dep")
@@ -442,8 +442,6 @@
     for r in range(NRAD):
         for c in range(3):
             out_v[c, rows(r)] = vel[ADJ, 1, c, R0 + r, LO:HI]
-    out_vel = pltpu.make_async_copy(out_v.at[pl.ds(0, 3)], adj_h.at[pl.ds(0, 3)], out_sem.at[0])
-    out_vel.start()
 
     def product(e, f):
         return 2.0 * DT * (e[0] * f[0] + e[1] * f[1] + e[2] * f[2]
@@ -459,16 +457,12 @@
             change = gm * e[i] + common if i < 3 else gm * e[i]
             out_v[3 + i, rows(r)] = a2[i, r] + change
         a1[ADJ, 0, r] = product(e, [strain[FWD, 0, i, r] for i in range(6)])
-    out_stress = pltpu.make_async_copy(out_v.at[pl.ds(3, 6)], adj_h.at[pl.ds(3, 6)], out_sem.at[1])
-    out_stress.start()
 
     arrive(legs_v[FWD])
     parcel = wraps(FWD, 3, VEL_AHEAD)
     for r in range(NRAD):
         e = strain_at(FWD, 1, parcel, r)
         grad_v[rows(r)] = a1[ADJ, 0, r] + product(e, [strain[ADJ, 0, i, r] for i in range(6)])
-    out_grad = pltpu.make_async_copy(grad_v, grad_h, out_sem.at[2])
-    out_grad.start()
 
     for legs, up_legs, dn_legs in started:
         for make in legs:
@@ -486,16 +480,10 @@
             for make in dn_legs:
                 make().wait_send()
 
-    out_vel.wait()
-    out_stress.wait()
-    out_grad.wait()
-
 
 def hand_on(grad_in, adj_in, grad_out, adj_out, sems):
-    copies = [
-        pltpu.make_async_copy(adj_in.at[pl.ds(3 * i, 3)], adj_out.at[pl.ds(3 * i, 3)], sems.at[i])
-        for i in range(3)
-    ] + [pltpu.make_async_copy(grad_in, grad_out, sems.at[3])]
+    copies = [pltpu.make_async_copy(adj_in, adj_out, sems.at[0]),
+              pltpu.make_async_copy(grad_in, grad_out, sems.at[1])]
     for copy in copies:
         copy.start()
     for copy in copies:
@@ -514,12 +502,9 @@
     hbm = pl.BlockSpec(memory_space=pltpu.HBM)
     gradient, adjoint_out = pl.pallas_call(
         kernel,
-        out_shape=(
-            jax.ShapeDtypeStruct((cells, LANES), f32),
-            jax.ShapeDtypeStruct((9, cells, LANES), f32),
-        ),
+        out_shape=(vmem((cells, LANES), f32), vmem((9, cells, LANES), f32)),
         in_specs=[hbm] * 13,
-        out_specs=(hbm, hbm),
+        out_specs=(pl.BlockSpec(memory_space=pltpu.VMEM),) * 2,
         scratch_shapes=[
             vmem((2, 9, cells, LANES), f32),
             vmem((2, 18, cells, LANES), f32),
@@ -543,10 +528,7 @@
             vmem((2, 2, 3) + block, f32),
             vmem((4,) + block, f32),
             vmem((8,) + block, f32),
-            vmem((9, cells, LANES), f32),
-            vmem((cells, LANES), f32),
             pltpu.SemaphoreType.DMA((16,)),
-            pltpu.SemaphoreType.DMA((3,)),
             pltpu.SemaphoreType.DMA((2, 4, 7)),
             pltpu.SemaphoreType.DMA((2, 4, 7)),
         ],
@@ -571,10 +553,10 @@
             jax.ShapeDtypeStruct((cells, LANES), f32),
             jax.ShapeDtypeStruct((9, cells, LANES), f32),
         ),
-        in_specs=[hbm, hbm],
+        in_specs=[pl.BlockSpec(memory_space=pl.ANY)] * 2,
         out_specs=(hbm, hbm),
-        scratch_shapes=[pltpu.SemaphoreType.DMA((4,))],
-        compiler_params=pltpu.CompilerParams(vmem_limit_bytes=60 * 2**20),
+        scratch_shapes=[pltpu.SemaphoreType.DMA((2,))],
+        compiler_params=pltpu.CompilerParams(vmem_limit_bytes=2**20),
         name="hand_on",
     )(gradient, adjoint_out)
     return gradient.reshape(NAZ, NRAD, LANES), adjoint_out.reshape(9, NAZ, NRAD, LANES)

time: 36.6 us -> 25.7 us (0.70)
  Pallas kernels: 35.7 us -> 24.8 us
    pallas_call x1, Pallas kernels: 11.1 us -> 0.73 us  [shards(): pl.pallas_call(hand_on, out_shape=(jax.ShapeDtypeStruct((cells, LANES), f...]
    pallas_call x1, Pallas kernels: 24.6 us -> 24.1 us  [shards(): pl.pallas_call(kernel, out_shape=(vmem((cells, LANES), f32), vmem((9, cel...]
where the time goes in v2:
time: 25.7 us; the launch traced here: 25.5 us
  Pallas kernels  24.8 us (96%)
  between operations  0.64 us (2%)
    pallas_call x1, Pallas kernels, shards(): pl.pallas_call(kernel, out_shape=(vmem((cells, LANES), f32), vmem((9, cel...  24.1 us
    pallas_call x1, Pallas kernels, shards(): pl.pallas_call(hand_on, out_shape=(jax.ShapeDtypeStruct((cells, LANES), f...  0.73 us

profile of v2, /device:TPU:32, one launch (start us, length us, event | category | flops | bytes accessed | tf_op | source)
XLA Modules:
  0.0 25.5 jit_solution(1253876336240535549)
XLA Ops:
  0.6 24.1 %window.1 = (f32[64,128]{1,0:T(8,128)S(1)}, f32[9,64,128]{2,1,0:T(8,128)S(1)}) custom-call(f32[9,64,128]{2,1,0:T(8,128)} %bitcast.14, f32[18,64,128]{2,1,0:T(8,128)} %bitcast.12, f32[9,64,128]{2,1,0:T(8,128)} %bitcast.15, f32[18,64,128]{2,1,0:T(8,128)} %bitcast.13, f32[64,128]{1,0:T(8,128)} %bitcast.16, s32[64,128]{1,0:T(8,128)} %bitcast.17, f32[2,8]{1,0:T(2,128)} %ze_h.1, ...), custom_call_target="tpu_custom_call" | custom-call | tf_op jit(solution)/shard_map/window/pallas_call | solution.py:503
  24.7 0.7 %hand_on.1 = (f32[64,128]{1,0:T(8,128)}, f32[9,64,128]{2,1,0:T(8,128)}) custom-call(f32[64,128]{1,0:T(8,128)S(1)} %get-tuple-element.6.grad_in, f32[9,64,128]{2,1,0:T(8,128)S(1)} %get-tuple-element.7.adj_in), custom_call_target="tpu_custom_call" | custom-call | tf_op jit(solution)/shard_map/hand_on/pallas_call | solution.py:550

commit v3 on v2

--- a/solution.py
+++ b/solution.py
@@ -50,7 +50,7 @@
     fs, fm, as_, am, mu_h, zone_h, ze_h, zr_h, zw_h, sc_h, sf_h, rc_h, rr_h,
     grad_v, out_v,
     raw, mem, mu_v, zone_v, ze, zr, zw, sc_v, sf_v, rc_v, rr_v,
-    stress, vel, dz, msg_out, msg_in, strain, a1, a2, inj, geo, mat,
+    stress, vel, dz, az_out, az_in, msg_out, msg_in, strain, a1, a2, inj, geo, mat,
     in_sem, send_sem, recv_sem,
 ):
     n_az, n_rad, n_dep = lax.axis_size("az"), lax.axis_size("rad"), lax.axis_size("dep")
@@ -164,20 +164,19 @@
         return dz[sys, t, r] + jnp.concatenate(halves, axis=0)
 
     own = pl.ds(LO, NAZ)
-    own_r = pl.ds(R0, NRAD)
     started = []
 
-    def exchange(sys, phase, field, rad_plan, az_from, az_count):
+    def exchange(sys, phase, field, rad_plan, az_from, gets):
         number = [0]
         legs, up_legs, dn_legs = [], [], []
 
-        def leg(where, src, dst, place, group):
+        def leg(src, dst, place, group):
             n = number[0]
             number[0] += 1
 
             def make():
                 return pltpu.make_async_remote_copy(
-                    src_ref=where.slab(src), dst_ref=where.slab(dst),
+                    src_ref=src(), dst_ref=dst(),
                     send_sem=send_sem.at[sys, phase, n], recv_sem=recv_sem.at[sys, phase, n],
                     device_id=place, device_id_type=MESH,
                 )
@@ -185,42 +184,41 @@
             make().start()
             group.append(make)
 
+        def layers(first, count, start, size):
+            return lambda: field.slab((pl.ds(first, count), pl.ds(start, size), own))
+
         @pl.when(has_up)
         def _():
             for first, count, up, down in rad_plan:
-                comps = pl.ds(first, count)
-                leg(field, (comps, pl.ds(R0 + NRAD - up, up), own), (comps, pl.ds(R0 - up, up), own),
+                leg(layers(first, count, R0 + NRAD - up, up), layers(first, count, R0 - up, up),
                     rad_up, up_legs)
 
         @pl.when(has_dn)
         def _():
             for first, count, up, down in rad_plan:
-                comps = pl.ds(first, count)
-                leg(field, (comps, pl.ds(R0, down), own), (comps, pl.ds(R0 + NRAD, down), own),
+                leg(layers(first, count, R0, down), layers(first, count, R0 + NRAD, down),
                     rad_dn, dn_legs)
 
-        comps = pl.ds(az_from, az_count)
-        leg(field, (comps, own_r, pl.ds(HI - 8, 8)), (comps, own_r, pl.ds(0, 8)), az_up, legs)
-        leg(field, (comps, own_r, pl.ds(LO, 8)), (comps, own_r, pl.ds(HI, 8)), az_dn, legs)
-        legs_msg = number[0]
-
-        def make_depth():
-            return pltpu.make_async_remote_copy(
-                src_ref=msg_out.at[sys, phase], dst_ref=msg_in.at[sys, phase],
-                send_sem=send_sem.at[sys, phase, legs_msg], recv_sem=recv_sem.at[sys, phase, legs_msg],
-                device_id=dep_other, device_id_type=MESH,
-            )
-
-        make_depth().start()
-        legs.append(make_depth)
-        groups = legs, up_legs, dn_legs
+        for way, row, place in ((0, HI - 2, az_up), (1, LO, az_dn)):
+            for i in range(3):
+                for r in range(NRAD):
+                    az_out[sys, phase, way, i, 2 * r: 2 * r + 2] = field[az_from + i, R0 + r, row: row + 2]
+            leg(lambda way=way: az_out.at[sys, phase, way], lambda way=way: az_in.at[sys, phase, way],
+                place, legs)
+        pack_depth(sys, phase, gets)
+        leg(lambda: msg_out.at[sys, phase], lambda: msg_in.at[sys, phase], dep_other, legs)
+        groups = legs, up_legs, dn_legs, (sys, phase, field, az_from)
         started.append(groups)
         return groups
 
     def arrive(groups):
-        legs, up_legs, dn_legs = groups
+        legs, up_legs, dn_legs, (sys, phase, field, az_from) = groups
         for make in legs:
             make().wait_recv()
+        for way, row in ((0, LO - 2), (1, HI)):
+            for i in range(3):
+                for r in range(NRAD):
+                    field[az_from + i, R0 + r, row: row + 2] = az_in[sys, phase, way, i, 2 * r: 2 * r + 2]
 
         @pl.when(has_dn)
         def _():
@@ -247,16 +245,14 @@
     def send_stress(sys, step):
         field = stress_field(sys, step)
         gets = [lambda r, c=c: field[c, R0 + r, LO:HI] for c in (RZ, TZ, ZZ)]
-        pack_depth(sys, 2 * step, gets)
-        groups = exchange(sys, 2 * step, field, ((RR, 1, 1, 2), (RZ, 2, 2, 1)), RT, 3)
+        groups = exchange(sys, 2 * step, field, ((RR, 1, 1, 2), (RZ, 2, 2, 1)), RT, gets)
         local_depth(sys, gets, STRESS_AHEAD)
         return groups
 
     def send_vel(sys, step):
         field = vel_field(sys, step)
         gets = [lambda r, c=c: field[c, R0 + r, LO:HI] for c in (2, 0, 1)]
-        pack_depth(sys, 2 * step + 1, gets)
-        groups = exchange(sys, 2 * step + 1, field, ((0, 1, 2, 1), (1, 2, 1, 2)), 0, 3)
+        groups = exchange(sys, 2 * step + 1, field, ((0, 1, 2, 1), (1, 2, 1, 2)), 0, gets)
         local_depth(sys, gets, VEL_AHEAD)
         return groups
 
@@ -464,19 +460,19 @@
         e = strain_at(FWD, 1, parcel, r)
         grad_v[rows(r)] = a1[ADJ, 0, r] + product(e, [strain[ADJ, 0, i, r] for i in range(6)])
 
-    for legs, up_legs, dn_legs in started:
+    for legs, _, _, _ in started:
         for make in legs:
             make().wait_send()
 
     @pl.when(has_up)
     def _():
-        for _, up_legs, _ in started:
+        for _, up_legs, _, _ in started:
             for make in up_legs:
                 make().wait_send()
 
     @pl.when(has_dn)
     def _():
-        for _, _, dn_legs in started:
+        for _, _, dn_legs, _ in started:
             for make in dn_legs:
                 make().wait_send()
 
@@ -520,6 +516,8 @@
             vmem((2, 2, 6, NRAD + 4, NAZ + 16, LANES), f32),
             vmem((2, 2, 3, NRAD + 4, NAZ + 16, LANES), f32),
             vmem((2, 3) + block, f32),
+            vmem((2, 4, 2, 3, 8, LANES), f32),
+            vmem((2, 4, 2, 3, 8, LANES), f32),
             vmem((2, 4, 8, LANES), f32),
             vmem((2, 4, 8, LANES), f32),
             vmem((2, 1, 6) + block, f32),

time: 25.7 us -> 24.8 us (0.965)
  Pallas kernels: 24.8 us -> 24 us
    pallas_call x1, Pallas kernels: 24.1 us -> 23.3 us  [shards(): pl.pallas_call(kernel, out_shape=(vmem((cells, LANES), f32), vmem((9, cel...]
where the time goes in v3:
time: 24.8 us; the launch traced here: 24.7 us
  Pallas kernels  24 us (97%)
  between operations  0.64 us (3%)
    pallas_call x1, Pallas kernels, shards(): pl.pallas_call(kernel, out_shape=(vmem((cells, LANES), f32), vmem((9, cel...  23.3 us
    pallas_call x1, Pallas kernels, shards(): pl.pallas_call(hand_on, out_shape=(jax.ShapeDtypeStruct((cells, LANES), f...  0.73 us

profile of v3, /device:TPU:32, one launch (start us, length us, event | category | flops | bytes accessed | tf_op | source)
XLA Modules:
  0.0 24.7 jit_solution(198561044651523245)
XLA Ops:
  0.6 23.3 %window.1 = (f32[64,128]{1,0:T(8,128)S(1)}, f32[9,64,128]{2,1,0:T(8,128)S(1)}) custom-call(f32[9,64,128]{2,1,0:T(8,128)} %bitcast.14, f32[18,64,128]{2,1,0:T(8,128)} %bitcast.12, f32[9,64,128]{2,1,0:T(8,128)} %bitcast.15, f32[18,64,128]{2,1,0:T(8,128)} %bitcast.13, f32[64,128]{1,0:T(8,128)} %bitcast.16, s32[64,128]{1,0:T(8,128)} %bitcast.17, f32[2,8]{1,0:T(2,128)} %ze_h.1, ...), custom_call_target="tpu_custom_call" | custom-call | tf_op jit(solution)/shard_map/window/pallas_call | solution.py:499
  23.9 0.7 %hand_on.1 = (f32[64,128]{1,0:T(8,128)}, f32[9,64,128]{2,1,0:T(8,128)}) custom-call(f32[64,128]{1,0:T(8,128)S(1)} %get-tuple-element.6.grad_in, f32[9,64,128]{2,1,0:T(8,128)S(1)} %get-tuple-element.7.adj_in), custom_call_target="tpu_custom_call" | custom-call | tf_op jit(solution)/shard_map/hand_on/pallas_call | solution.py:548

commit v4 on v3

--- a/solution.py
+++ b/solution.py
@@ -21,7 +21,8 @@
 ADJ, FWD = 0, 1
 NAZ, NRAD, LANES = 16, 4, 128
 LO, HI = 8, 8 + NAZ
-R0 = 2
+STRESS_PLAN = (((RR, 3), (RZ, 2), (RZ, 3), (RT, 2), (RT, 3)), ((RR, 0), (RR, 1), (RZ, 0), (RT, 0)))
+VEL_PLAN = (((0, 2), (0, 3), (1, 3), (2, 3)), ((0, 0), (1, 0), (1, 1), (2, 0), (2, 1)))
 
 
 class View:
@@ -33,9 +34,6 @@
 
     def __setitem__(self, index, value):
         self.ref[self.lead + index] = value
-
-    def slab(self, index):
-        return self.ref.at[self.lead + index]
 
 
 def forward4(before, here, after, after2):
@@ -50,7 +48,7 @@
     fs, fm, as_, am, mu_h, zone_h, ze_h, zr_h, zw_h, sc_h, sf_h, rc_h, rr_h,
     grad_v, out_v,
     raw, mem, mu_v, zone_v, ze, zr, zw, sc_v, sf_v, rc_v, rr_v,
-    stress, vel, dz, az_out, az_in, msg_out, msg_in, strain, a1, a2, inj, geo, mat,
+    stress, vel, dz, rad_out, rad_in, az_out, az_in, msg_out, msg_in, strain, a1, a2, inj, geo, mat,
     in_sem, send_sem, recv_sem,
 ):
     n_az, n_rad, n_dep = lax.axis_size("az"), lax.axis_size("rad"), lax.axis_size("dep")
@@ -92,7 +90,6 @@
         )
     ]
     got_vel = [bring(states[s].at[pl.ds(0, 3)], raw.at[s, pl.ds(0, 3)]) for s in (ADJ, FWD)]
-    got_mem = [bring(memories[s], mem.at[s]) for s in (ADJ, FWD)]
 
     lane = lax.broadcasted_iota(jnp.int32, (NAZ, LANES), 1)
     lane8 = lax.broadcasted_iota(jnp.int32, (8, LANES), 1)
@@ -163,10 +160,19 @@
             halves.append(jnp.where(edge, piece, 0.0))
         return dz[sys, t, r] + jnp.concatenate(halves, axis=0)
 
-    own = pl.ds(LO, NAZ)
     started = []
 
-    def exchange(sys, phase, field, rad_plan, az_from, gets):
+    def plan_of(phase):
+        return VEL_PLAN if phase % 2 else STRESS_PLAN
+
+    def keep(sys, phase, c, r, value):
+        ref = vel if phase % 2 else stress
+        ref[sys, phase // 2, c, r, LO:HI] = value
+        for way in range(2):
+            if (c, r) in plan_of(phase)[way]:
+                rad_out[sys, phase, way, plan_of(phase)[way].index((c, r))] = value
+
+    def exchange(sys, phase, field, az_from, gets):
         number = [0]
         legs, up_legs, dn_legs = [], [], []
 
@@ -184,25 +190,21 @@
             make().start()
             group.append(make)
 
-        def layers(first, count, start, size):
-            return lambda: field.slab((pl.ds(first, count), pl.ds(start, size), own))
+        def layers(ref, way):
+            return lambda: ref.at[sys, phase, way, pl.ds(0, len(plan_of(phase)[way]))]
 
         @pl.when(has_up)
         def _():
-            for first, count, up, down in rad_plan:
-                leg(layers(first, count, R0 + NRAD - up, up), layers(first, count, R0 - up, up),
-                    rad_up, up_legs)
+            leg(layers(rad_out, 0), layers(rad_in, 0), rad_up, up_legs)
 
         @pl.when(has_dn)
         def _():
-            for first, count, up, down in rad_plan:
-                leg(layers(first, count, R0, down), layers(first, count, R0 + NRAD, down),
-                    rad_dn, dn_legs)
+            leg(layers(rad_out, 1), layers(rad_in, 1), rad_dn, dn_legs)
 
         for way, row, place in ((0, HI - 2, az_up), (1, LO, az_dn)):
             for i in range(3):
                 for r in range(NRAD):
-                    az_out[sys, phase, way, i, 2 * r: 2 * r + 2] = field[az_from + i, R0 + r, row: row + 2]
+                    az_out[sys, phase, way, i, 2 * r: 2 * r + 2] = field[az_from + i, r, row: row + 2]
             leg(lambda way=way: az_out.at[sys, phase, way], lambda way=way: az_in.at[sys, phase, way],
                 place, legs)
         pack_depth(sys, phase, gets)
@@ -218,7 +220,7 @@
         for way, row in ((0, LO - 2), (1, HI)):
             for i in range(3):
                 for r in range(NRAD):
-                    field[az_from + i, R0 + r, row: row + 2] = az_in[sys, phase, way, i, 2 * r: 2 * r + 2]
+                    field[az_from + i, r, row: row + 2] = az_in[sys, phase, way, i, 2 * r: 2 * r + 2]
 
         @pl.when(has_dn)
         def _():
@@ -244,67 +246,76 @@
 
     def send_stress(sys, step):
         field = stress_field(sys, step)
-        gets = [lambda r, c=c: field[c, R0 + r, LO:HI] for c in (RZ, TZ, ZZ)]
-        groups = exchange(sys, 2 * step, field, ((RR, 1, 1, 2), (RZ, 2, 2, 1)), RT, gets)
+        gets = [lambda r, c=c: field[c, r, LO:HI] for c in (RZ, TZ, ZZ)]
+        groups = exchange(sys, 2 * step, field, RT, gets)
         local_depth(sys, gets, STRESS_AHEAD)
         return groups
 
     def send_vel(sys, step):
         field = vel_field(sys, step)
-        gets = [lambda r, c=c: field[c, R0 + r, LO:HI] for c in (2, 0, 1)]
-        groups = exchange(sys, 2 * step + 1, field, ((0, 1, 2, 1), (1, 2, 1, 2)), 0, gets)
+        gets = [lambda r, c=c: field[c, r, LO:HI] for c in (2, 0, 1)]
+        groups = exchange(sys, 2 * step + 1, field, 0, gets)
         local_depth(sys, gets, VEL_AHEAD)
         return groups
 
-    def rad4(field, c, r, first):
-        return [field[c, R0 + r + first + i, LO:HI] for i in range(4)]
+    def rad4(sys, phase, c, r, first):
+        field = vel if phase % 2 else stress
+        up, down = plan_of(phase)
+        found = []
+        for k in range(r + first, r + first + 4):
+            if k < 0:
+                found.append(rad_in[sys, phase, 0, up.index((c, k + NRAD))])
+            elif k >= NRAD:
+                found.append(rad_in[sys, phase, 1, down.index((c, k - NRAD))])
+            else:
+                found.append(field[sys, phase // 2, c, k, LO:HI])
+        return found
 
     def az4(field, c, r, first):
-        return [field[c, R0 + r, LO + first + i: HI + first + i] for i in range(4)]
+        return [field[c, r, LO + first + i: HI + first + i] for i in range(4)]
 
     def velocity_update(sys, step):
-        field, new = stress_field(sys, step), vel_field(sys, step)
+        field = stress_field(sys, step)
         parcel = wraps(sys, 2 * step, STRESS_AHEAD)
         for r in range(NRAD):
             inv_s, inv_c, inv_sa, inv_ca = [geo[i, r] for i in range(4)]
             if step == 0:
                 old = [raw[sys, c, rows(r)] for c in range(3)]
             else:
-                old = [vel[sys, 0, c, R0 + r, LO:HI] for c in range(3)]
-            s_rr, s_tt = field[RR, R0 + r, LO:HI], field[TT, R0 + r, LO:HI]
-            s_rt, s_rz = field[RT, R0 + r, LO:HI], field[RZ, R0 + r, LO:HI]
+                old = [vel[sys, 0, c, r, LO:HI] for c in range(3)]
+            s_rr, s_tt = field[RR, r, LO:HI], field[TT, r, LO:HI]
+            s_rt, s_rz = field[RT, r, LO:HI], field[RZ, r, LO:HI]
             push = [
-                forward4(*rad4(field, RR, r, -1)) + backward4(*az4(field, RT, r, -2)) * inv_sa
+                forward4(*rad4(sys, 2 * step, RR, r, -1)) + backward4(*az4(field, RT, r, -2)) * inv_sa
                 + depth_diff(sys, parcel, 0, r) + (s_rr - s_tt) * inv_s,
-                backward4(*rad4(field, RT, r, -2)) + forward4(*az4(field, TT, r, -1)) * inv_ca
+                backward4(*rad4(sys, 2 * step, RT, r, -2)) + forward4(*az4(field, TT, r, -1)) * inv_ca
                 + depth_diff(sys, parcel, 1, r) + 2.0 * s_rt * inv_c,
-                backward4(*rad4(field, RZ, r, -2)) + backward4(*az4(field, TZ, r, -2)) * inv_ca
+                backward4(*rad4(sys, 2 * step, RZ, r, -2)) + backward4(*az4(field, TZ, r, -2)) * inv_ca
                 + depth_diff(sys, parcel, 2, r) + s_rz * inv_c,
             ]
             gain = mat[0, r]
             for c in range(3):
-                new[c, R0 + r, LO:HI] = old[c] + gain * (push[c] + inj[sys, step, c, r])
+                keep(sys, 2 * step + 1, c, r, old[c] + gain * (push[c] + inj[sys, step, c, r]))
 
     def strain_at(sys, step, parcel, r):
         field = vel_field(sys, step)
         inv_s, inv_c, inv_sa, inv_ca = [geo[i, r] for i in range(4)]
-        v_r, v_t = field[0, R0 + r, LO:HI], field[1, R0 + r, LO:HI]
+        v_r, v_t = field[0, r, LO:HI], field[1, r, LO:HI]
         return [
-            backward4(*rad4(field, 0, r, -2)),
+            backward4(*rad4(sys, 2 * step + 1, 0, r, -2)),
             backward4(*az4(field, 1, r, -2)) * inv_ca + v_r * inv_c,
             depth_diff(sys, parcel, 0, r),
-            0.5 * (forward4(*rad4(field, 1, r, -1)) + forward4(*az4(field, 0, r, -1)) * inv_sa
+            0.5 * (forward4(*rad4(sys, 2 * step + 1, 1, r, -1)) + forward4(*az4(field, 0, r, -1)) * inv_sa
                    - v_t * inv_s),
-            0.5 * (depth_diff(sys, parcel, 1, r) + forward4(*rad4(field, 2, r, -1))),
+            0.5 * (depth_diff(sys, parcel, 1, r) + forward4(*rad4(sys, 2 * step + 1, 2, r, -1))),
             0.5 * (depth_diff(sys, parcel, 2, r) + forward4(*az4(field, 2, r, -1)) * inv_ca),
         ]
 
     def load_state(sys):
         got_stress[sys].wait()
-        field = stress_field(sys, 0)
         for c in range(6):
             for r in range(NRAD):
-                field[c, R0 + r, LO:HI] = raw[sys, IN_STATE[c], rows(r)]
+                keep(sys, 0, c, r, raw[sys, IN_STATE[c], rows(r)])
 
     load_state(ADJ)
     pl.semaphore_wait(barrier, 3 + has_up.astype(jnp.int32) + has_dn.astype(jnp.int32))
@@ -313,20 +324,15 @@
     legs_s[ADJ] = send_stress(ADJ, 0)
     load_state(FWD)
     legs_s[FWD] = send_stress(FWD, 0)
+    got_mem = [bring(memories[s], mem.at[s]) for s in (ADJ, FWD)]
 
     @pl.when(rad == 0)
     def _():
-        for sys in (ADJ, FWD):
-            for step in range(2):
-                stress[sys, step, 0:3, 0:R0, LO:HI] = jnp.zeros((3, R0, NAZ, LANES), f32)
-                vel[sys, step, :, 0:R0, LO:HI] = jnp.zeros((3, R0, NAZ, LANES), f32)
+        rad_in[:, :, 0] = jnp.zeros((2, 4, 5, NAZ, LANES), f32)
 
     @pl.when(rad == n_rad - 1)
     def _():
-        for sys in (ADJ, FWD):
-            for step in range(2):
-                stress[sys, step, 0:3, R0 + NRAD:, LO:HI] = jnp.zeros((3, 2, NAZ, LANES), f32)
-                vel[sys, step, :, R0 + NRAD:, LO:HI] = jnp.zeros((3, 2, NAZ, LANES), f32)
+        rad_in[:, :, 1] = jnp.zeros((2, 4, 5, NAZ, LANES), f32)
 
     for copy in got_small:
         copy.wait()
@@ -410,7 +416,6 @@
     def first_stress(sys):
         arrive(legs_v[sys])
         parcel = wraps(sys, 1, VEL_AHEAD)
-        new = stress_field(sys, 1)
         for r in range(NRAD):
             e = strain_at(sys, 0, parcel, r)
             dilation = e[0] + e[1] + e[2]
@@ -419,7 +424,7 @@
             for i in range(6):
                 strain[sys, 0, i, r] = e[i]
                 change = gm * e[i] + common if i < 3 else gm * e[i]
-                new[STRAIN_ORDER[i], R0 + r, LO:HI] = a1[sys, i, r] + change
+                keep(sys, 2, STRAIN_ORDER[i], r, a1[sys, i, r] + change)
         legs_s[sys] = send_stress(sys, 1)
 
     for sys in (ADJ, FWD):
@@ -431,13 +436,13 @@
         hm = mat[4, r]
         for i in range(6):
             drop = hm * e[i] + common if i < 3 else hm * e[i]
-            a2[i, r] = stress[ADJ, 1, STRAIN_ORDER[i], R0 + r, LO:HI] - a2[i, r] - drop
+            a2[i, r] = stress[ADJ, 1, STRAIN_ORDER[i], r, LO:HI] - a2[i, r] - drop
 
     for sys in (ADJ, FWD):
         advance_velocity(sys, 1)
     for r in range(NRAD):
         for c in range(3):
-            out_v[c, rows(r)] = vel[ADJ, 1, c, R0 + r, LO:HI]
+            out_v[c, rows(r)] = vel[ADJ, 1, c, r, LO:HI]
 
     def product(e, f):
         return 2.0 * DT * (e[0] * f[0] + e[1] * f[1] + e[2] * f[2]
@@ -513,9 +518,11 @@
             vmem((3, 2, nsrc), f32),
             vmem((1, nrec), jnp.int32),
             vmem((3, 2, nrec), f32),
-            vmem((2, 2, 6, NRAD + 4, NAZ + 16, LANES), f32),
-            vmem((2, 2, 3, NRAD + 4, NAZ + 16, LANES), f32),
+            vmem((2, 2, 6, NRAD, NAZ + 16, LANES), f32),
+            vmem((2, 2, 3, NRAD, NAZ + 16, LANES), f32),
             vmem((2, 3) + block, f32),
+            vmem((2, 4, 2, 5, NAZ, LANES), f32),
+            vmem((2, 4, 2, 5, NAZ, LANES), f32),
             vmem((2, 4, 2, 3, 8, LANES), f32),
             vmem((2, 4, 2, 3, 8, LANES), f32),
             vmem((2, 4, 8, LANES), f32),
@@ -527,8 +534,8 @@
             vmem((4,) + block, f32),
             vmem((8,) + block, f32),
             pltpu.SemaphoreType.DMA((16,)),
-            pltpu.SemaphoreType.DMA((2, 4, 7)),
-            pltpu.SemaphoreType.DMA((2, 4, 7)),
+            pltpu.SemaphoreType.DMA((2, 4, 5)),
+            pltpu.SemaphoreType.DMA((2, 4, 5)),
         ],
         compiler_params=pltpu.CompilerParams(
             collective_id=0, has_side_effects=True, vmem_limit_bytes=60 * 2**20

time: 24.8 us -> 24.4 us (0.984)
  Pallas kernels: 24 us -> 23.6 us
    pallas_call x1, Pallas kernels: 23.3 us -> 22.9 us  [shards(): pl.pallas_call(kernel, out_shape=(vmem((cells, LANES), f32), vmem((9, cel...]
where the time goes in v4:
time: 24.4 us; the launch traced here: 24.3 us
  Pallas kernels  23.6 us (97%)
  between operations  0.64 us (3%)
    pallas_call x1, Pallas kernels, shards(): pl.pallas_call(kernel, out_shape=(vmem((cells, LANES), f32), vmem((9, cel...  22.9 us
    pallas_call x1, Pallas kernels, shards(): pl.pallas_call(hand_on, out_shape=(jax.ShapeDtypeStruct((cells, LANES), f...  0.73 us

profile of v4, /device:TPU:32, one launch (start us, length us, event | category | flops | bytes accessed | tf_op | source)
XLA Modules:
  0.0 24.3 jit_solution(13331954836235004347)
XLA Ops:
  0.6 22.9 %window.1 = (f32[64,128]{1,0:T(8,128)S(1)}, f32[9,64,128]{2,1,0:T(8,128)S(1)}) custom-call(f32[9,64,128]{2,1,0:T(8,128)} %bitcast.14, f32[18,64,128]{2,1,0:T(8,128)} %bitcast.12, f32[9,64,128]{2,1,0:T(8,128)} %bitcast.15, f32[18,64,128]{2,1,0:T(8,128)} %bitcast.13, f32[64,128]{1,0:T(8,128)} %bitcast.16, s32[64,128]{1,0:T(8,128)} %bitcast.17, f32[2,8]{1,0:T(2,128)} %ze_h.1, ...), custom_call_target="tpu_custom_call" | custom-call | tf_op jit(solution)/shard_map/window/pallas_call | solution.py:504
  23.5 0.7 %hand_on.1 = (f32[64,128]{1,0:T(8,128)}, f32[9,64,128]{2,1,0:T(8,128)}) custom-call(f32[64,128]{1,0:T(8,128)S(1)} %get-tuple-element.6.grad_in, f32[9,64,128]{2,1,0:T(8,128)S(1)} %get-tuple-element.7.adj_in), custom_call_target="tpu_custom_call" | custom-call | tf_op jit(solution)/shard_map/hand_on/pallas_call | solution.py:555

commit v5 on v4

--- a/solution.py
+++ b/solution.py
@@ -25,6 +25,10 @@
 VEL_PLAN = (((0, 2), (0, 3), (1, 3), (2, 3)), ((0, 0), (1, 0), (1, 1), (2, 0), (2, 1)))
 
 
+STRESS_AHEAD, VEL_AHEAD = (False, False, True), (False, True, True)
+STRESS_AZ_AHEAD, VEL_AZ_AHEAD = (False, True, False), (True, False, True)
+
+
 class View:
     def __init__(self, ref, sys, step):
         self.ref, self.lead = ref, (sys, step)
@@ -48,8 +52,8 @@
     fs, fm, as_, am, mu_h, zone_h, ze_h, zr_h, zw_h, sc_h, sf_h, rc_h, rr_h,
     grad_v, out_v,
     raw, mem, mu_v, zone_v, ze, zr, zw, sc_v, sf_v, rc_v, rr_v,
-    stress, vel, dz, rad_out, rad_in, az_out, az_in, msg_out, msg_in, strain, a1, a2, inj, geo, mat,
-    in_sem, send_sem, recv_sem,
+    stress, vel, acc, azc, rad_out, rad_in, crit_out, crit_in, gain_in, beside, az_out, az_in, msg_out, msg_in, strain, a1, a2, inj, geo, mat,
+    in_sem, send_sem, recv_sem, gain_sem,
 ):
     n_az, n_rad, n_dep = lax.axis_size("az"), lax.axis_size("rad"), lax.axis_size("dep")
     az, rad, dep = lax.axis_index("az"), lax.axis_index("rad"), lax.axis_index("dep")
@@ -81,15 +85,6 @@
     states = (as_, fs)
     memories = (am, fm)
     got_stress = [bring(states[s].at[pl.ds(3, 6)], raw.at[s, pl.ds(3, 6)]) for s in (ADJ, FWD)]
-
-    got_small = [
-        bring(a, b)
-        for a, b in (
-            (ze_h, ze), (zr_h, zr), (zw_h, zw), (sc_h, sc_v), (sf_h, sf_v), (rc_h, rc_v),
-            (rr_h, rr_v), (zone_h, zone_v), (mu_h, mu_v),
-        )
-    ]
-    got_vel = [bring(states[s].at[pl.ds(0, 3)], raw.at[s, pl.ds(0, 3)]) for s in (ADJ, FWD)]
 
     lane = lax.broadcasted_iota(jnp.int32, (NAZ, LANES), 1)
     lane8 = lax.broadcasted_iota(jnp.int32, (8, LANES), 1)
@@ -114,20 +109,16 @@
                     parcel = piece if parcel is None else parcel + piece
         msg_out[sys, phase] = parcel
 
-    def local_depth(sys, gets, aheads):
-        for t in range(3):
-            for r in range(NRAD):
-                g = gets[t](r)
-                m1 = pltpu.roll(g, LANES - 1, 1)
-                r1 = pltpu.roll(g, 1, 1)
-                if aheads[t]:
-                    m2 = pltpu.roll(g, LANES - 2, 1)
-                    dz[sys, t, r] = (where_f(lane < 127, C1) * m1 - C1 * g - where_f(lane < 126, C2) * m2
-                                     + where_f(lane >= 1, C2) * r1)
-                else:
-                    r2 = pltpu.roll(g, 2, 1)
-                    dz[sys, t, r] = (C1 * g - where_f(lane >= 1, C1) * r1 - where_f(lane < 127, C2) * m1
-                                     + where_f(lane >= 2, C2) * r2)
+    def depth_local(g, ahead):
+        m1 = pltpu.roll(g, LANES - 1, 1)
+        r1 = pltpu.roll(g, 1, 1)
+        if ahead:
+            m2 = pltpu.roll(g, LANES - 2, 1)
+            return (where_f(lane < 127, C1) * m1 - C1 * g - where_f(lane < 126, C2) * m2
+                    + where_f(lane >= 1, C2) * r1)
+        r2 = pltpu.roll(g, 2, 1)
+        return (C1 * g - where_f(lane >= 1, C1) * r1 - where_f(lane < 127, C2) * m1
+                + where_f(lane >= 2, C2) * r2)
 
     slot = lax.rem(lax.rem(lane8 + 2, LANES), 12)
     place_in = lax.rem(slot, 4)
@@ -152,13 +143,13 @@
     mine = lane8 - 126 * (1 - dep)
     edge = (mine >= 0) & (mine < 2)
 
-    def depth_diff(sys, parcel, t, r):
+    def depth_halo(parcel, t, r):
         halves = []
         for half in range(2):
             shift = base(t, r, half)
             piece = pltpu.roll(parcel, LANES - shift, 1) if shift else parcel
             halves.append(jnp.where(edge, piece, 0.0))
-        return dz[sys, t, r] + jnp.concatenate(halves, axis=0)
+        return jnp.concatenate(halves, axis=0)
 
     started = []
 
@@ -168,6 +159,8 @@
     def keep(sys, phase, c, r, value):
         ref = vel if phase % 2 else stress
         ref[sys, phase // 2, c, r, LO:HI] = value
+        if phase % 2:
+            return
         for way in range(2):
             if (c, r) in plan_of(phase)[way]:
                 rad_out[sys, phase, way, plan_of(phase)[way].index((c, r))] = value
@@ -190,17 +183,20 @@
             make().start()
             group.append(make)
 
-        def layers(ref, way):
-            return lambda: ref.at[sys, phase, way, pl.ds(0, len(plan_of(phase)[way]))]
+        def radial(way, out):
+            if phase % 2:
+                return (crit_out if out else crit_in).at[sys, phase // 2, way]
+            return (rad_out if out else rad_in).at[sys, phase, way, pl.ds(0, len(plan_of(phase)[way]))]
 
         @pl.when(has_up)
         def _():
-            leg(layers(rad_out, 0), layers(rad_in, 0), rad_up, up_legs)
+            leg(lambda: radial(0, True), lambda: radial(0, False), rad_up, up_legs)
 
         @pl.when(has_dn)
         def _():
-            leg(layers(rad_out, 1), layers(rad_in, 1), rad_dn, dn_legs)
-
+            leg(lambda: radial(1, True), lambda: radial(1, False), rad_dn, dn_legs)
+
+        yield None
         for way, row, place in ((0, HI - 2, az_up), (1, LO, az_dn)):
             for i in range(3):
                 for r in range(NRAD):
@@ -209,18 +205,105 @@
                 place, legs)
         pack_depth(sys, phase, gets)
         leg(lambda: msg_out.at[sys, phase], lambda: msg_in.at[sys, phase], dep_other, legs)
-        groups = legs, up_legs, dn_legs, (sys, phase, field, az_from)
+        groups = legs, up_legs, dn_legs, (sys, phase)
         started.append(groups)
-        return groups
+        yield groups
+
+    def radial_pair(make):
+        @pl.when(has_up)
+        def _():
+            make(0).start()
+
+        @pl.when(has_dn)
+        def _():
+            make(1).start()
+
+        started.append(([], [lambda: make(0)], [lambda: make(1)], (None, 0)))
+        return make
+
+    def landed(make):
+        @pl.when(has_dn)
+        def _():
+            make(0).wait_recv()
+
+        @pl.when(has_up)
+        def _():
+            make(1).wait_recv()
+
+    def send_gain():
+        return radial_pair(lambda way: pltpu.make_async_remote_copy(
+            src_ref=mat.at[0, pl.ds(2 * (1 - way), 2)], dst_ref=gain_in.at[way],
+            send_sem=gain_sem.at[0, way], recv_sem=gain_sem.at[1, way],
+            device_id=(rad_up, rad_dn)[way], device_id_type=MESH,
+        ))
+
+    def send_ahead(sys, step):
+        phase = 2 * step + 1
+        for way in range(2):
+            for i, (c, r) in enumerate(VEL_PLAN[way]):
+                rad_out[sys, phase, way, i] = acc[sys, c, r]
+
+        def make(way):
+            count = pl.ds(0, len(VEL_PLAN[way]))
+            return pltpu.make_async_remote_copy(
+                src_ref=rad_out.at[sys, phase, way, count], dst_ref=rad_in.at[sys, phase, way, count],
+                send_sem=send_sem.at[sys, phase, 5 + way], recv_sem=recv_sem.at[sys, phase, 5 + way],
+                device_id=(rad_up, rad_dn)[way], device_id_type=MESH,
+            )
+
+        return radial_pair(make)
+
+    PUSHED_BY = ((RR, True), (RT, False), (RZ, False))
+
+    def rebuild(sys, step, ahead_copies):
+        landed(ahead_copies)
+        phase = 2 * step + 1
+        for way in range(2):
+            for i, (c, r) in enumerate(VEL_PLAN[way]):
+                comp, ahead = PUSHED_BY[c]
+                first = -1 if ahead else -2
+                total = None
+                for shift, factor in enumerate((C2, -C1, C1, -C2)):
+                    k = r + first + shift
+                    if 0 <= k < NRAD:
+                        continue
+                    term = factor * stress[sys, step, comp, k % NRAD, LO:HI]
+                    total = term if total is None else total + term
+                rad_in[sys, phase, way, i] = rad_in[sys, phase, way, i] + gain_in[way, r % 2] * total
+
+    def add_late(sys, step):
+        phase = 2 * step + 1
+        for way in range(2):
+            lanes_tile = crit_in[sys, step, way, 3]
+            for i, (c, r) in enumerate(VEL_PLAN[way]):
+                rad_in[sys, phase, way, i] = (rad_in[sys, phase, way, i]
+                                              + gain_in[way, r % 2] * depth_halo(lanes_tile, c, r))
+                for side, row in ((0, 0), (1, NAZ - 2)):
+                    source = 4 * side + 2 * (r % 2)
+                    rad_in[sys, phase, way, i, row: row + 2] = (
+                        rad_in[sys, phase, way, i, row: row + 2]
+                        + beside[way, 0 if c == 0 else 1, r % 2, row: row + 2]
+                        * crit_in[sys, step, way, c, source: source + 2])
+
+    even = lax.rem(lax.broadcasted_iota(jnp.int32, (8, LANES), 0), 2) == 0
 
     def arrive(groups):
-        legs, up_legs, dn_legs, (sys, phase, field, az_from) = groups
+        legs, up_legs, dn_legs, (sys, phase) = groups
         for make in legs:
             make().wait_recv()
-        for way, row in ((0, LO - 2), (1, HI)):
-            for i in range(3):
-                for r in range(NRAD):
-                    field[az_from + i, r, row: row + 2] = az_in[sys, phase, way, i, 2 * r: 2 * r + 2]
+        for i, ahead in enumerate(VEL_AZ_AHEAD if phase % 2 else STRESS_AZ_AHEAD):
+            low, high = az_in[sys, phase, 0, i], az_in[sys, phase, 1, i]
+            if ahead:
+                low = jnp.where(even, C2 * pltpu.roll(low, 7, 0), 0.0)
+                high = jnp.where(even, 0.0, C1 * pltpu.roll(high, 1, 0)) - C2 * high
+            else:
+                low = C2 * low - jnp.where(even, C1 * pltpu.roll(low, 7, 0), 0.0)
+                high = jnp.where(even, 0.0, -C2 * pltpu.roll(high, 1, 0))
+            az_in[sys, phase, 0, i] = low
+            az_in[sys, phase, 1, i] = high
+            for r in range(NRAD):
+                azc[sys, i, r, 0:2] = az_in[sys, phase, 0, i, 2 * r: 2 * r + 2]
+                azc[sys, i, r, NAZ - 2: NAZ] = az_in[sys, phase, 1, i, 2 * r: 2 * r + 2]
 
         @pl.when(has_dn)
         def _():
@@ -232,6 +315,9 @@
             for make in dn_legs:
                 make().wait_recv()
 
+        if phase % 2:
+            add_late(sys, phase // 2)
+
     def rows(r):
         return pl.ds(r, NAZ, stride=NRAD)
 
@@ -241,42 +327,64 @@
     def vel_field(sys, step):
         return View(vel, sys, step)
 
-    STRESS_AHEAD = (False, False, True)
-    VEL_AHEAD = (False, True, True)
+    def stress_gets(sys, step):
+        field = stress_field(sys, step)
+        return [lambda r, c=c: field[c, r, LO:HI] for c in (RZ, TZ, ZZ)]
+
+    def vel_gets(sys, step):
+        field = vel_field(sys, step)
+        return [lambda r, c=c: field[c, r, LO:HI] for c in (2, 0, 1)]
 
     def send_stress(sys, step):
-        field = stress_field(sys, step)
-        gets = [lambda r, c=c: field[c, r, LO:HI] for c in (RZ, TZ, ZZ)]
-        groups = exchange(sys, 2 * step, field, RT, gets)
-        local_depth(sys, gets, STRESS_AHEAD)
-        return groups
-
-    def send_vel(sys, step):
-        field = vel_field(sys, step)
-        gets = [lambda r, c=c: field[c, r, LO:HI] for c in (2, 0, 1)]
-        groups = exchange(sys, 2 * step + 1, field, 0, gets)
-        local_depth(sys, gets, VEL_AHEAD)
-        return groups
-
-    def rad4(sys, phase, c, r, first):
+        steps = exchange(sys, 2 * step, stress_field(sys, step), RT, stress_gets(sys, step))
+        next(steps)
+        return next(steps)
+
+    def start_vel(sys, step):
+        return exchange(sys, 2 * step + 1, vel_field(sys, step), 0, vel_gets(sys, step))
+
+    def rad_local(sys, phase, c, r, ahead):
         field = vel if phase % 2 else stress
+
+        def own(k):
+            return field[sys, phase // 2, c, k, LO:HI]
+
+        first = -1 if ahead else -2
+        factors = {first: C2, first + 1: -C1, first + 2: C1, first + 3: -C2}
+        total = None
+        for shift, factor in factors.items():
+            if 0 <= r + shift < NRAD:
+                term = factor * own(r + shift)
+                total = term if total is None else total + term
+        return total
+
+    def rad_halo(sys, phase, c, r, ahead):
         up, down = plan_of(phase)
-        found = []
-        for k in range(r + first, r + first + 4):
-            if k < 0:
-                found.append(rad_in[sys, phase, 0, up.index((c, k + NRAD))])
-            elif k >= NRAD:
-                found.append(rad_in[sys, phase, 1, down.index((c, k - NRAD))])
-            else:
-                found.append(field[sys, phase // 2, c, k, LO:HI])
-        return found
+        first = -1 if ahead else -2
+        factors = {first: C2, first + 1: -C1, first + 2: C1, first + 3: -C2}
+        total = None
+        for shift, factor in factors.items():
+            k = r + shift
+            if 0 <= k < NRAD:
+                continue
+            way, row = (0, up.index((c, k + NRAD))) if k < 0 else (1, down.index((c, k - NRAD)))
+            term = factor * rad_in[sys, phase, way, row]
+            total = term if total is None else total + term
+        return total
+
+    def plus(*terms):
+        terms = [t for t in terms if t is not None]
+        total = terms[0]
+        for t in terms[1:]:
+            total = total + t
+        return total
 
     def az4(field, c, r, first):
         return [field[c, r, LO + first + i: HI + first + i] for i in range(4)]
 
-    def velocity_update(sys, step):
-        field = stress_field(sys, step)
-        parcel = wraps(sys, 2 * step, STRESS_AHEAD)
+    def velocity_local(sys, step):
+        field, phase = stress_field(sys, step), 2 * step
+        gets = stress_gets(sys, step)
         for r in range(NRAD):
             inv_s, inv_c, inv_sa, inv_ca = [geo[i, r] for i in range(4)]
             if step == 0:
@@ -286,30 +394,65 @@
             s_rr, s_tt = field[RR, r, LO:HI], field[TT, r, LO:HI]
             s_rt, s_rz = field[RT, r, LO:HI], field[RZ, r, LO:HI]
             push = [
-                forward4(*rad4(sys, 2 * step, RR, r, -1)) + backward4(*az4(field, RT, r, -2)) * inv_sa
-                + depth_diff(sys, parcel, 0, r) + (s_rr - s_tt) * inv_s,
-                backward4(*rad4(sys, 2 * step, RT, r, -2)) + forward4(*az4(field, TT, r, -1)) * inv_ca
-                + depth_diff(sys, parcel, 1, r) + 2.0 * s_rt * inv_c,
-                backward4(*rad4(sys, 2 * step, RZ, r, -2)) + backward4(*az4(field, TZ, r, -2)) * inv_ca
-                + depth_diff(sys, parcel, 2, r) + s_rz * inv_c,
+                rad_local(sys, phase, RR, r, True) + backward4(*az4(field, RT, r, -2)) * inv_sa
+                + depth_local(gets[0](r), False) + (s_rr - s_tt) * inv_s,
+                rad_local(sys, phase, RT, r, False) + forward4(*az4(field, TT, r, -1)) * inv_ca
+                + depth_local(gets[1](r), False) + 2.0 * s_rt * inv_c,
+                rad_local(sys, phase, RZ, r, False) + backward4(*az4(field, TZ, r, -2)) * inv_ca
+                + depth_local(gets[2](r), True) + s_rz * inv_c,
             ]
             gain = mat[0, r]
             for c in range(3):
-                keep(sys, 2 * step + 1, c, r, old[c] + gain * (push[c] + inj[sys, step, c, r]))
+                acc[sys, c, r] = old[c] + gain * (push[c] + inj[sys, step, c, r])
+
+    def velocity_finish(sys, step):
+        phase = 2 * step
+        parcel = wraps(sys, phase, STRESS_AHEAD)
+        for way in range(2):
+            start = 4 * (1 - way)
+            for c in range(3):
+                for side in range(2):
+                    crit_out[sys, step, way, c, 4 * side: 4 * side + 4] = (
+                        az_in[sys, phase, side, c, start: start + 4])
+            crit_out[sys, step, way, 3] = parcel
+        steps = start_vel(sys, step)
+        next(steps)
+        for r in range(NRAD):
+            gain = mat[0, r]
+            inv = (geo[2, r], geo[3, r], geo[3, r])
+            for c, (s, ahead) in enumerate(PUSHED_BY):
+                halo = plus(azc[sys, c, r] * inv[c], depth_halo(parcel, c, r),
+                            rad_halo(sys, phase, s, r, ahead))
+                keep(sys, phase + 1, c, r, acc[sys, c, r] + gain * halo)
+        return next(steps)
+
+    def strain_local(sys, step):
+        field, phase = vel_field(sys, step), 2 * step + 1
+        gets = vel_gets(sys, step)
+        for r in range(NRAD):
+            inv_s, inv_c, inv_sa, inv_ca = [geo[i, r] for i in range(4)]
+            v_r, v_t = field[0, r, LO:HI], field[1, r, LO:HI]
+            acc[sys, 0, r] = rad_local(sys, phase, 0, r, False)
+            acc[sys, 1, r] = backward4(*az4(field, 1, r, -2)) * inv_ca + v_r * inv_c
+            acc[sys, 2, r] = depth_local(gets[0](r), False)
+            acc[sys, 3, r] = 0.5 * (rad_local(sys, phase, 1, r, True)
+                                    + forward4(*az4(field, 0, r, -1)) * inv_sa - v_t * inv_s)
+            acc[sys, 4, r] = 0.5 * (depth_local(gets[1](r), True) + rad_local(sys, phase, 2, r, True))
+            acc[sys, 5, r] = 0.5 * (depth_local(gets[2](r), True)
+                                    + forward4(*az4(field, 2, r, -1)) * inv_ca)
 
     def strain_at(sys, step, parcel, r):
-        field = vel_field(sys, step)
-        inv_s, inv_c, inv_sa, inv_ca = [geo[i, r] for i in range(4)]
-        v_r, v_t = field[0, r, LO:HI], field[1, r, LO:HI]
-        return [
-            backward4(*rad4(sys, 2 * step + 1, 0, r, -2)),
-            backward4(*az4(field, 1, r, -2)) * inv_ca + v_r * inv_c,
-            depth_diff(sys, parcel, 0, r),
-            0.5 * (forward4(*rad4(sys, 2 * step + 1, 1, r, -1)) + forward4(*az4(field, 0, r, -1)) * inv_sa
-                   - v_t * inv_s),
-            0.5 * (depth_diff(sys, parcel, 1, r) + forward4(*rad4(sys, 2 * step + 1, 2, r, -1))),
-            0.5 * (depth_diff(sys, parcel, 2, r) + forward4(*az4(field, 2, r, -1)) * inv_ca),
+        phase = 2 * step + 1
+        inv_sa, inv_ca = geo[2, r], geo[3, r]
+        halo = [
+            rad_halo(sys, phase, 0, r, False),
+            azc[sys, 1, r] * inv_ca,
+            depth_halo(parcel, 0, r),
+            0.5 * plus(azc[sys, 0, r] * inv_sa, rad_halo(sys, phase, 1, r, True)),
+            0.5 * plus(depth_halo(parcel, 1, r), rad_halo(sys, phase, 2, r, True)),
+            0.5 * (depth_halo(parcel, 2, r) + azc[sys, 2, r] * inv_ca),
         ]
+        return [plus(acc[sys, i, r], halo[i]) for i in range(6)]
 
     def load_state(sys):
         got_stress[sys].wait()
@@ -321,18 +464,31 @@
     pl.semaphore_wait(barrier, 3 + has_up.astype(jnp.int32) + has_dn.astype(jnp.int32))
     legs_s = [None, None]
     legs_v = [None, None]
+    ahead = [None, None]
     legs_s[ADJ] = send_stress(ADJ, 0)
     load_state(FWD)
     legs_s[FWD] = send_stress(FWD, 0)
+    got_small = [
+        bring(a, b)
+        for a, b in (
+            (ze_h, ze), (zr_h, zr), (zw_h, zw), (sc_h, sc_v), (sf_h, sf_v), (rc_h, rc_v),
+            (rr_h, rr_v), (zone_h, zone_v), (mu_h, mu_v),
+        )
+    ]
+    got_vel = [bring(states[s].at[pl.ds(0, 3)], raw.at[s, pl.ds(0, 3)]) for s in (ADJ, FWD)]
     got_mem = [bring(memories[s], mem.at[s]) for s in (ADJ, FWD)]
 
     @pl.when(rad == 0)
     def _():
         rad_in[:, :, 0] = jnp.zeros((2, 4, 5, NAZ, LANES), f32)
+        crit_in[:, :, 0] = jnp.zeros((2, 2, 4, 8, LANES), f32)
+        gain_in[0] = jnp.zeros((2, NAZ, LANES), f32)
 
     @pl.when(rad == n_rad - 1)
     def _():
         rad_in[:, :, 1] = jnp.zeros((2, 4, 5, NAZ, LANES), f32)
+        crit_in[:, :, 1] = jnp.zeros((2, 2, 4, 8, LANES), f32)
+        gain_in[1] = jnp.zeros((2, NAZ, LANES), f32)
 
     for copy in got_small:
         copy.wait()
@@ -371,6 +527,8 @@
         for i in range(3):
             mat[5 + i, r] = beta[i]
 
+    gains = send_gain()
+
     def inject(sys, cells_ref, force_ref, count):
         cells = cells_ref[...]
         around = lax.shift_right_logical(cells, 13) - NAZ * az
@@ -394,14 +552,30 @@
     inject(FWD, sc_v, sf_v, sc_v.shape[1])
     for sys in (ADJ, FWD):
         got_vel[sys].wait()
+        azc[sys] = jnp.zeros((3, NRAD, NAZ, LANES), f32)
+        for step in range(2):
+            for row in (0, HI):
+                stress[sys, step, RT: RT + 3, :, row: row + 8] = jnp.zeros((3, NRAD, 8, LANES), f32)
+                vel[sys, step, :, :, row: row + 8] = jnp.zeros((3, NRAD, 8, LANES), f32)
+        velocity_local(sys, 0)
+        ahead[sys] = send_ahead(sys, 0)
 
     def advance_velocity(sys, step):
         arrive(legs_s[sys])
-        velocity_update(sys, step)
-        legs_v[sys] = send_vel(sys, step)
+        legs_v[sys] = velocity_finish(sys, step)
 
     for sys in (ADJ, FWD):
         advance_velocity(sys, 0)
+    landed(gains)
+    for way in range(2):
+        for r in range(2):
+            layer = (rad * NRAD + (r - 2 if way == 0 else NRAD + r)).astype(f32)
+            centre = jnp.full((NAZ, LANES), f32(inner), f32) + layer
+            beside[way, 0, r] = gain_in[way, r] / ((centre + 0.5) * angle)
+            beside[way, 1, r] = gain_in[way, r] / (centre * angle)
+    for sys in (ADJ, FWD):
+        rebuild(sys, 0, ahead[sys])
+        strain_local(sys, 0)
 
     for sys in (ADJ, FWD):
         got_mem[sys].wait()
@@ -429,6 +603,9 @@
 
     for sys in (ADJ, FWD):
         first_stress(sys)
+    for sys in (ADJ, FWD):
+        velocity_local(sys, 1)
+        ahead[sys] = send_ahead(sys, 1)
 
     for r in range(NRAD):
         e = [strain[ADJ, 0, i, r] for i in range(6)]
@@ -440,6 +617,9 @@
 
     for sys in (ADJ, FWD):
         advance_velocity(sys, 1)
+    for sys in (ADJ, FWD):
+        rebuild(sys, 1, ahead[sys])
+        strain_local(sys, 1)
     for r in range(NRAD):
         for c in range(3):
             out_v[c, rows(r)] = vel[ADJ, 1, c, r, LO:HI]
@@ -448,6 +628,24 @@
         return 2.0 * DT * (e[0] * f[0] + e[1] * f[1] + e[2] * f[2]
                            + 2.0 * (e[3] * f[3] + e[4] * f[4] + e[5] * f[5]))
 
+    def sent(batch):
+        for legs, _, _, _ in batch:
+            for make in legs:
+                make().wait_send()
+
+        @pl.when(has_up)
+        def _():
+            for _, up_legs, _, _ in batch:
+                for make in up_legs:
+                    make().wait_send()
+
+        @pl.when(has_dn)
+        def _():
+            for _, _, dn_legs, _ in batch:
+                for make in dn_legs:
+                    make().wait_send()
+
+    sent([g for g in started if g[3][1] != 3])
     arrive(legs_v[ADJ])
     parcel = wraps(ADJ, 3, VEL_AHEAD)
     for r in range(NRAD):
@@ -465,21 +663,7 @@
         e = strain_at(FWD, 1, parcel, r)
         grad_v[rows(r)] = a1[ADJ, 0, r] + product(e, [strain[ADJ, 0, i, r] for i in range(6)])
 
-    for legs, _, _, _ in started:
-        for make in legs:
-            make().wait_send()
-
-    @pl.when(has_up)
-    def _():
-        for _, up_legs, _, _ in started:
-            for make in up_legs:
-                make().wait_send()
-
-    @pl.when(has_dn)
-    def _():
-        for _, _, dn_legs, _ in started:
-            for make in dn_legs:
-                make().wait_send()
+    sent([g for g in started if g[3][1] == 3])
 
 
 def hand_on(grad_in, adj_in, grad_out, adj_out, sems):
@@ -520,9 +704,14 @@
             vmem((3, 2, nrec), f32),
             vmem((2, 2, 6, NRAD, NAZ + 16, LANES), f32),
             vmem((2, 2, 3, NRAD, NAZ + 16, LANES), f32),
+            vmem((2, 6) + block, f32),
             vmem((2, 3) + block, f32),
             vmem((2, 4, 2, 5, NAZ, LANES), f32),
             vmem((2, 4, 2, 5, NAZ, LANES), f32),
+            vmem((2, 2, 2, 4, 8, LANES), f32),
+            vmem((2, 2, 2, 4, 8, LANES), f32),
+            vmem((2, 2, NAZ, LANES), f32),
+            vmem((2, 2, 2, NAZ, LANES), f32),
             vmem((2, 4, 2, 3, 8, LANES), f32),
             vmem((2, 4, 2, 3, 8, LANES), f32),
             vmem((2, 4, 8, LANES), f32),
@@ -534,8 +723,9 @@
             vmem((4,) + block, f32),
             vmem((8,) + block, f32),
             pltpu.SemaphoreType.DMA((16,)),
-            pltpu.SemaphoreType.DMA((2, 4, 5)),
-            pltpu.SemaphoreType.DMA((2, 4, 5)),
+            pltpu.SemaphoreType.DMA((2, 4, 7)),
+            pltpu.SemaphoreType.DMA((2, 4, 7)),
+            pltpu.SemaphoreType.DMA((2, 2)),
         ],
         compiler_params=pltpu.CompilerParams(
             collective_id=0, has_side_effects=True, vmem_limit_bytes=60 * 2**20

time: 24.4 us -> 24.3 us (level)
    pallas_call x1, Pallas kernels: 22.9 us -> 22.6 us  [shards(): pl.pallas_call(kernel, out_shape=(vmem((cells, LANES), f32), vmem((9, cel...]
where the time goes in v5:
time: 24.3 us; the launch traced here: 24 us
  Pallas kernels  23.4 us (96%)
  between operations  0.64 us (3%)
    pallas_call x1, Pallas kernels, shards(): pl.pallas_call(kernel, out_shape=(vmem((cells, LANES), f32), vmem((9, cel...  22.6 us
    pallas_call x1, Pallas kernels, shards(): pl.pallas_call(hand_on, out_shape=(jax.ShapeDtypeStruct((cells, LANES), f...  0.73 us

profile of v5, /device:TPU:32, one launch (start us, length us, event | category | flops | bytes accessed | tf_op | source)
XLA Modules:
  0.0 24.0 jit_solution(16055175458245266643)
XLA Ops:
  0.6 22.6 %window.1 = (f32[64,128]{1,0:T(8,128)S(1)}, f32[9,64,128]{2,1,0:T(8,128)S(1)}) custom-call(f32[9,64,128]{2,1,0:T(8,128)} %bitcast.14, f32[18,64,128]{2,1,0:T(8,128)} %bitcast.12, f32[9,64,128]{2,1,0:T(8,128)} %bitcast.15, f32[18,64,128]{2,1,0:T(8,128)} %bitcast.13, f32[64,128]{1,0:T(8,128)} %bitcast.16, s32[64,128]{1,0:T(8,128)} %bitcast.17, f32[2,8]{1,0:T(2,128)} %ze_h.1, ...), custom_call_target="tpu_custom_call" | custom-call | tf_op jit(solution)/shard_map/window/pallas_call | solution.py:688
  23.3 0.7 %hand_on.1 = (f32[64,128]{1,0:T(8,128)}, f32[9,64,128]{2,1,0:T(8,128)}) custom-call(f32[64,128]{1,0:T(8,128)S(1)} %get-tuple-element.6.grad_in, f32[9,64,128]{2,1,0:T(8,128)S(1)} %get-tuple-element.7.adj_in), custom_call_target="tpu_custom_call" | custom-call | tf_op jit(solution)/shard_map/hand_on/pallas_call | solution.py:745

commit v6 on v5

--- a/solution.py
+++ b/solution.py
@@ -52,8 +52,8 @@
     fs, fm, as_, am, mu_h, zone_h, ze_h, zr_h, zw_h, sc_h, sf_h, rc_h, rr_h,
     grad_v, out_v,
     raw, mem, mu_v, zone_v, ze, zr, zw, sc_v, sf_v, rc_v, rr_v,
-    stress, vel, acc, azc, rad_out, rad_in, crit_out, crit_in, gain_in, beside, az_out, az_in, msg_out, msg_in, strain, a1, a2, inj, geo, mat,
-    in_sem, send_sem, recv_sem, gain_sem,
+    stress, vel, acc, azc, rad_out, rad_in, az_out, az_in, msg_out, msg_in, strain, a1, a2, inj, geo, mat,
+    in_sem, send_sem, recv_sem,
 ):
     n_az, n_rad, n_dep = lax.axis_size("az"), lax.axis_size("rad"), lax.axis_size("dep")
     az, rad, dep = lax.axis_index("az"), lax.axis_index("rad"), lax.axis_index("dep")
@@ -159,8 +159,6 @@
     def keep(sys, phase, c, r, value):
         ref = vel if phase % 2 else stress
         ref[sys, phase // 2, c, r, LO:HI] = value
-        if phase % 2:
-            return
         for way in range(2):
             if (c, r) in plan_of(phase)[way]:
                 rad_out[sys, phase, way, plan_of(phase)[way].index((c, r))] = value
@@ -183,20 +181,17 @@
             make().start()
             group.append(make)
 
-        def radial(way, out):
-            if phase % 2:
-                return (crit_out if out else crit_in).at[sys, phase // 2, way]
-            return (rad_out if out else rad_in).at[sys, phase, way, pl.ds(0, len(plan_of(phase)[way]))]
+        def layers(ref, way):
+            return lambda: ref.at[sys, phase, way, pl.ds(0, len(plan_of(phase)[way]))]
 
         @pl.when(has_up)
         def _():
-            leg(lambda: radial(0, True), lambda: radial(0, False), rad_up, up_legs)
+            leg(layers(rad_out, 0), layers(rad_in, 0), rad_up, up_legs)
 
         @pl.when(has_dn)
         def _():
-            leg(lambda: radial(1, True), lambda: radial(1, False), rad_dn, dn_legs)
-
-        yield None
+            leg(layers(rad_out, 1), layers(rad_in, 1), rad_dn, dn_legs)
+
         for way, row, place in ((0, HI - 2, az_up), (1, LO, az_dn)):
             for i in range(3):
                 for r in range(NRAD):
@@ -207,83 +202,7 @@
         leg(lambda: msg_out.at[sys, phase], lambda: msg_in.at[sys, phase], dep_other, legs)
         groups = legs, up_legs, dn_legs, (sys, phase)
         started.append(groups)
-        yield groups
-
-    def radial_pair(make):
-        @pl.when(has_up)
-        def _():
-            make(0).start()
-
-        @pl.when(has_dn)
-        def _():
-            make(1).start()
-
-        started.append(([], [lambda: make(0)], [lambda: make(1)], (None, 0)))
-        return make
-
-    def landed(make):
-        @pl.when(has_dn)
-        def _():
-            make(0).wait_recv()
-
-        @pl.when(has_up)
-        def _():
-            make(1).wait_recv()
-
-    def send_gain():
-        return radial_pair(lambda way: pltpu.make_async_remote_copy(
-            src_ref=mat.at[0, pl.ds(2 * (1 - way), 2)], dst_ref=gain_in.at[way],
-            send_sem=gain_sem.at[0, way], recv_sem=gain_sem.at[1, way],
-            device_id=(rad_up, rad_dn)[way], device_id_type=MESH,
-        ))
-
-    def send_ahead(sys, step):
-        phase = 2 * step + 1
-        for way in range(2):
-            for i, (c, r) in enumerate(VEL_PLAN[way]):
-                rad_out[sys, phase, way, i] = acc[sys, c, r]
-
-        def make(way):
-            count = pl.ds(0, len(VEL_PLAN[way]))
-            return pltpu.make_async_remote_copy(
-                src_ref=rad_out.at[sys, phase, way, count], dst_ref=rad_in.at[sys, phase, way, count],
-                send_sem=send_sem.at[sys, phase, 5 + way], recv_sem=recv_sem.at[sys, phase, 5 + way],
-                device_id=(rad_up, rad_dn)[way], device_id_type=MESH,
-            )
-
-        return radial_pair(make)
-
-    PUSHED_BY = ((RR, True), (RT, False), (RZ, False))
-
-    def rebuild(sys, step, ahead_copies):
-        landed(ahead_copies)
-        phase = 2 * step + 1
-        for way in range(2):
-            for i, (c, r) in enumerate(VEL_PLAN[way]):
-                comp, ahead = PUSHED_BY[c]
-                first = -1 if ahead else -2
-                total = None
-                for shift, factor in enumerate((C2, -C1, C1, -C2)):
-                    k = r + first + shift
-                    if 0 <= k < NRAD:
-                        continue
-                    term = factor * stress[sys, step, comp, k % NRAD, LO:HI]
-                    total = term if total is None else total + term
-                rad_in[sys, phase, way, i] = rad_in[sys, phase, way, i] + gain_in[way, r % 2] * total
-
-    def add_late(sys, step):
-        phase = 2 * step + 1
-        for way in range(2):
-            lanes_tile = crit_in[sys, step, way, 3]
-            for i, (c, r) in enumerate(VEL_PLAN[way]):
-                rad_in[sys, phase, way, i] = (rad_in[sys, phase, way, i]
-                                              + gain_in[way, r % 2] * depth_halo(lanes_tile, c, r))
-                for side, row in ((0, 0), (1, NAZ - 2)):
-                    source = 4 * side + 2 * (r % 2)
-                    rad_in[sys, phase, way, i, row: row + 2] = (
-                        rad_in[sys, phase, way, i, row: row + 2]
-                        + beside[way, 0 if c == 0 else 1, r % 2, row: row + 2]
-                        * crit_in[sys, step, way, c, source: source + 2])
+        return groups
 
     even = lax.rem(lax.broadcasted_iota(jnp.int32, (8, LANES), 0), 2) == 0
 
@@ -315,9 +234,6 @@
             for make in dn_legs:
                 make().wait_recv()
 
-        if phase % 2:
-            add_late(sys, phase // 2)
-
     def rows(r):
         return pl.ds(r, NAZ, stride=NRAD)
 
@@ -336,11 +252,9 @@
         return [lambda r, c=c: field[c, r, LO:HI] for c in (2, 0, 1)]
 
     def send_stress(sys, step):
-        steps = exchange(sys, 2 * step, stress_field(sys, step), RT, stress_gets(sys, step))
-        next(steps)
-        return next(steps)
-
-    def start_vel(sys, step):
+        return exchange(sys, 2 * step, stress_field(sys, step), RT, stress_gets(sys, step))
+
+    def send_vel(sys, step):
         return exchange(sys, 2 * step + 1, vel_field(sys, step), 0, vel_gets(sys, step))
 
     def rad_local(sys, phase, c, r, ahead):
@@ -408,23 +322,13 @@
     def velocity_finish(sys, step):
         phase = 2 * step
         parcel = wraps(sys, phase, STRESS_AHEAD)
-        for way in range(2):
-            start = 4 * (1 - way)
-            for c in range(3):
-                for side in range(2):
-                    crit_out[sys, step, way, c, 4 * side: 4 * side + 4] = (
-                        az_in[sys, phase, side, c, start: start + 4])
-            crit_out[sys, step, way, 3] = parcel
-        steps = start_vel(sys, step)
-        next(steps)
         for r in range(NRAD):
             gain = mat[0, r]
             inv = (geo[2, r], geo[3, r], geo[3, r])
-            for c, (s, ahead) in enumerate(PUSHED_BY):
+            for c, (s, ahead) in enumerate(((RR, True), (RT, False), (RZ, False))):
                 halo = plus(azc[sys, c, r] * inv[c], depth_halo(parcel, c, r),
                             rad_halo(sys, phase, s, r, ahead))
                 keep(sys, phase + 1, c, r, acc[sys, c, r] + gain * halo)
-        return next(steps)
 
     def strain_local(sys, step):
         field, phase = vel_field(sys, step), 2 * step + 1
@@ -464,7 +368,6 @@
     pl.semaphore_wait(barrier, 3 + has_up.astype(jnp.int32) + has_dn.astype(jnp.int32))
     legs_s = [None, None]
     legs_v = [None, None]
-    ahead = [None, None]
     legs_s[ADJ] = send_stress(ADJ, 0)
     load_state(FWD)
     legs_s[FWD] = send_stress(FWD, 0)
@@ -481,14 +384,10 @@
     @pl.when(rad == 0)
     def _():
         rad_in[:, :, 0] = jnp.zeros((2, 4, 5, NAZ, LANES), f32)
-        crit_in[:, :, 0] = jnp.zeros((2, 2, 4, 8, LANES), f32)
-        gain_in[0] = jnp.zeros((2, NAZ, LANES), f32)
 
     @pl.when(rad == n_rad - 1)
     def _():
         rad_in[:, :, 1] = jnp.zeros((2, 4, 5, NAZ, LANES), f32)
-        crit_in[:, :, 1] = jnp.zeros((2, 2, 4, 8, LANES), f32)
-        gain_in[1] = jnp.zeros((2, NAZ, LANES), f32)
 
     for copy in got_small:
         copy.wait()
@@ -527,8 +426,6 @@
         for i in range(3):
             mat[5 + i, r] = beta[i]
 
-    gains = send_gain()
-
     def inject(sys, cells_ref, force_ref, count):
         cells = cells_ref[...]
         around = lax.shift_right_logical(cells, 13) - NAZ * az
@@ -558,23 +455,15 @@
                 stress[sys, step, RT: RT + 3, :, row: row + 8] = jnp.zeros((3, NRAD, 8, LANES), f32)
                 vel[sys, step, :, :, row: row + 8] = jnp.zeros((3, NRAD, 8, LANES), f32)
         velocity_local(sys, 0)
-        ahead[sys] = send_ahead(sys, 0)
 
     def advance_velocity(sys, step):
         arrive(legs_s[sys])
-        legs_v[sys] = velocity_finish(sys, step)
+        velocity_finish(sys, step)
+        legs_v[sys] = send_vel(sys, step)
 
     for sys in (ADJ, FWD):
         advance_velocity(sys, 0)
-    landed(gains)
-    for way in range(2):
-        for r in range(2):
-            layer = (rad * NRAD + (r - 2 if way == 0 else NRAD + r)).astype(f32)
-            centre = jnp.full((NAZ, LANES), f32(inner), f32) + layer
-            beside[way, 0, r] = gain_in[way, r] / ((centre + 0.5) * angle)
-            beside[way, 1, r] = gain_in[way, r] / (centre * angle)
-    for sys in (ADJ, FWD):
-        rebuild(sys, 0, ahead[sys])
+    for sys in (ADJ, FWD):
         strain_local(sys, 0)
 
     for sys in (ADJ, FWD):
@@ -605,7 +494,6 @@
         first_stress(sys)
     for sys in (ADJ, FWD):
         velocity_local(sys, 1)
-        ahead[sys] = send_ahead(sys, 1)
 
     for r in range(NRAD):
         e = [strain[ADJ, 0, i, r] for i in range(6)]
@@ -618,7 +506,6 @@
     for sys in (ADJ, FWD):
         advance_velocity(sys, 1)
     for sys in (ADJ, FWD):
-        rebuild(sys, 1, ahead[sys])
         strain_local(sys, 1)
     for r in range(NRAD):
         for c in range(3):
@@ -645,7 +532,7 @@
                 for make in dn_legs:
                     make().wait_send()
 
-    sent([g for g in started if g[3][1] != 3])
+    sent(started[:6])
     arrive(legs_v[ADJ])
     parcel = wraps(ADJ, 3, VEL_AHEAD)
     for r in range(NRAD):
@@ -663,7 +550,7 @@
         e = strain_at(FWD, 1, parcel, r)
         grad_v[rows(r)] = a1[ADJ, 0, r] + product(e, [strain[ADJ, 0, i, r] for i in range(6)])
 
-    sent([g for g in started if g[3][1] == 3])
+    sent(started[6:])
 
 
 def hand_on(grad_in, adj_in, grad_out, adj_out, sems):
@@ -708,10 +595,6 @@
             vmem((2, 3) + block, f32),
             vmem((2, 4, 2, 5, NAZ, LANES), f32),
             vmem((2, 4, 2, 5, NAZ, LANES), f32),
-            vmem((2, 2, 2, 4, 8, LANES), f32),
-            vmem((2, 2, 2, 4, 8, LANES), f32),
-            vmem((2, 2, NAZ, LANES), f32),
-            vmem((2, 2, 2, NAZ, LANES), f32),
             vmem((2, 4, 2, 3, 8, LANES), f32),
             vmem((2, 4, 2, 3, 8, LANES), f32),
             vmem((2, 4, 8, LANES), f32),
@@ -723,9 +606,8 @@
             vmem((4,) + block, f32),
             vmem((8,) + block, f32),
             pltpu.SemaphoreType.DMA((16,)),
-            pltpu.SemaphoreType.DMA((2, 4, 7)),
-            pltpu.SemaphoreType.DMA((2, 4, 7)),
-            pltpu.SemaphoreType.DMA((2, 2)),
+            pltpu.SemaphoreType.DMA((2, 4, 5)),
+            pltpu.SemaphoreType.DMA((2, 4, 5)),
         ],
         compiler_params=pltpu.CompilerParams(
             collective_id=0, has_side_effects=True, vmem_limit_bytes=60 * 2**20

time: 24.3 us -> 24.3 us (level)
  no operation moved by 1% of the time
where the time goes in v6:
time: 24.3 us; the launch traced here: 24.2 us
  Pallas kernels  23.6 us (97%)
  between operations  0.64 us (3%)
    pallas_call x1, Pallas kernels, shards(): pl.pallas_call(kernel, out_shape=(vmem((cells, LANES), f32), vmem((9, cel...  22.8 us
    pallas_call x1, Pallas kernels, shards(): pl.pallas_call(hand_on, out_shape=(jax.ShapeDtypeStruct((cells, LANES), f...  0.73 us

profile of v6, /device:TPU:32, one launch (start us, length us, event | category | flops | bytes accessed | tf_op | source)
XLA Modules:
  0.0 24.2 jit_solution(2226300106552282751)
XLA Ops:
  0.6 22.8 %window.1 = (f32[64,128]{1,0:T(8,128)S(1)}, f32[9,64,128]{2,1,0:T(8,128)S(1)}) custom-call(f32[9,64,128]{2,1,0:T(8,128)} %bitcast.14, f32[18,64,128]{2,1,0:T(8,128)} %bitcast.12, f32[9,64,128]{2,1,0:T(8,128)} %bitcast.15, f32[18,64,128]{2,1,0:T(8,128)} %bitcast.13, f32[64,128]{1,0:T(8,128)} %bitcast.16, s32[64,128]{1,0:T(8,128)} %bitcast.17, f32[2,8]{1,0:T(2,128)} %ze_h.1, ...), custom_call_target="tpu_custom_call" | custom-call | tf_op jit(solution)/shard_map/window/pallas_call | solution.py:575
  23.5 0.7 %hand_on.1 = (f32[64,128]{1,0:T(8,128)}, f32[9,64,128]{2,1,0:T(8,128)}) custom-call(f32[64,128]{1,0:T(8,128)S(1)} %get-tuple-element.6.grad_in, f32[9,64,128]{2,1,0:T(8,128)S(1)} %get-tuple-element.7.adj_in), custom_call_target="tpu_custom_call" | custom-call | tf_op jit(solution)/shard_map/hand_on/pallas_call | solution.py:627
